TPU v7x, 128 devices: a whole 4x4x4 slice. The times are simulated.
128 devices in a mesh: gx: 16 (over y, x), gy: 8 (over z, core).
Axes of the slice: x: 4, y: 4, z: 4, core: 2. Of those that a mesh axis runs over, the one named last changes fastest.
Arguments:
- orbitals: float32 [32, 128, 128, 128], P(None, 'gx', 'gy'), may hold values from -50 to 50
- potential: float32 [128, 128, 128], P('gx', 'gy'), may hold values from -1 to 1
Outputs:
- orthonormal: float32 [32, 128, 128, 128], P(None, 'gx', 'gy')
All inputs are finite; a program needn't handle non-finite values.
Results may differ from a plain program's by a relative error of at most 0.00022.
Values sent between devices are 32-bit elements; how exact they have to be, the bound alone decides.
No kernel may reach another device: no remote copies, remote signals or barrier semaphores. Data moves between devices by JAX's collectives and lax.ppermute only.
A program may use at most 256 MiB of HBM per device.

v0:
```python
import functools
import math

import jax
import jax.numpy as jnp
from jax import lax
from jax.experimental import pallas as pl
from jax.experimental.pallas import tpu as pltpu
from jax.sharding import PartitionSpec as P

DEG = 4
HALO = 2 * DEG
CENTER = 5.0
HALF_W = 4.0
NEAR = (2.0 / HALF_W) * -0.5 * (4.0 / 3.0)
FAR = (2.0 / HALF_W) * 0.5 / 12.0
DIAG_SCALE = 2.0 / HALF_W
DIAG_SHIFT = (2.0 / HALF_W) * (3 * 0.5 * 2.5 - CENTER)

GROUP = 8
PREP_VMEM = 59 * 2**20
CHUNKS = (1, 2, 1)
UNITS = ((0, 0, 1), (1, 0, 1), (1, 1, 1), (2, 0, 1))
AFTER = {1: 0, 3: 1}
RIDES = {}
ALONE = (1,)
FILTER_COST = 100
GY = ("gz", "core")
CORES = 2


def axis_count(axis):
    return math.prod(lax.axis_size(a) for a in ((axis,) if isinstance(axis, str) else axis))


def shift_perm(axis, step):
    count = axis_count(axis)
    return [(i, (i + step) % count) for i in range(count)]


def both_ways(low_part, high_part, axis):
    return (
        lax.ppermute(high_part, axis, shift_perm(axis, 1)),
        lax.ppermute(low_part, axis, shift_perm(axis, -1)),
    )


def reach(plane, cx, left):
    outside = max(HALO - plane, plane - (HALO + cx - 1), 0)
    return left - 2 * ((outside + 1) // 2)


def halo_planes(cx, late=False):
    planes = []
    for plane in range(2, cx + 2 * HALO - 2):
        if late and HALO <= plane < HALO + cx:
            continue
        planes.append((plane, reach(plane, cx, HALO)))
    return planes


def diag_planes(cx):
    return range(4, cx + 2 * HALO - 4)


def split_plane(plane, cx):
    if plane < HALO:
        return 0, plane
    if plane < HALO + cx:
        return 1, plane - HALO
    return 2, plane - HALO - cx


def tile_block(out_ref, at, block):
    out_ref[at : at + block.shape[1]] = jnp.swapaxes(block, 0, 1)


def first_tiles_kernel(groups, pieces, pot_ref, orb_ref, out_ref, pot_here, here, tiles, in_sems, out_sems):
    cx, cy, cz = pot_ref.shape
    pot_copy = pltpu.make_async_copy(pot_ref, pot_here, in_sems.at[groups * pieces])
    pot_copy.start()
    deep = cx // pieces
    parts = [(g, p) for g in range(groups) for p in range(pieces)]
    loads, stores = [], []
    for index, (g, p) in enumerate(parts):
        part = (pl.ds(GROUP * g, GROUP), pl.ds(deep * p, deep))
        loads.append(pltpu.make_async_copy(orb_ref.at[part], here.at[part], in_sems.at[index]))
        loads[-1].start()

    def store(index, start, size):
        rows = pl.ds(start, size)
        stores.append(pltpu.make_async_copy(tiles.at[rows], out_ref.at[rows], out_sems.at[index]))
        stores[-1].start()

    pot_copy.wait()
    tiles[groups * cx * cy :] = pot_here[...].reshape(cx * cy // 8, 8, cz)
    store(groups * pieces, groups * cx * cy, cx * cy // 8)
    for index, (g, p) in enumerate(parts):
        loads[index].wait()
        for x in range(deep * p, deep * (p + 1)):
            tile_block(tiles, g * cx * cy + x * cy, here[GROUP * g : GROUP * (g + 1), x])
        store(index, g * cx * cy + deep * p * cy, deep * cy)
    for copy in stores:
        copy.wait()


def first_tiles(orbitals, potential):
    _, cx, cy, cz = orbitals.shape
    groups, pieces = CHUNKS[0], 2
    tiles = (groups * cx * cy + cx * cy // 8, 8, cz)
    return pl.pallas_call(
        functools.partial(first_tiles_kernel, groups, pieces),
        out_shape=jax.ShapeDtypeStruct(tiles, jnp.float32),
        in_specs=[pl.BlockSpec(memory_space=pltpu.HBM)] * 2,
        out_specs=pl.BlockSpec(memory_space=pltpu.HBM),
        scratch_shapes=[
            pltpu.VMEM((cx, cy, cz), jnp.float32),
            pltpu.VMEM((groups * GROUP, cx, cy, cz), jnp.float32),
            pltpu.VMEM(tiles, jnp.float32),
            pltpu.SemaphoreType.DMA((groups * pieces + 1,)),
            pltpu.SemaphoreType.DMA((groups * pieces + 1,)),
        ],
        compiler_params=pltpu.CompilerParams(vmem_limit_bytes=PREP_VMEM),
        name="first_tiles",
    )(potential, orbitals)


def tiles_kernel(chunks, pot_ref, orb_ref, *out_refs):
    cx, cy, cz = pot_ref.shape
    group = 0
    for out_ref, groups in zip(out_refs, chunks):
        for g in range(groups):
            for x in range(cx):
                tile_block(out_ref, g * cx * cy + x * cy, orb_ref[GROUP * group : GROUP * (group + 1), x])
            group += 1
    out_refs[0][chunks[0] * cx * cy :] = pot_ref[...].reshape(cx * cy // 8, 8, cz)


def all_tiles(orbitals, potential):
    _, cx, cy, cz = orbitals.shape
    tiles = [groups * cx * cy for groups in CHUNKS]
    tiles[0] += cx * cy // 8
    return pl.pallas_call(
        functools.partial(tiles_kernel, CHUNKS),
        out_shape=[jax.ShapeDtypeStruct((t, 8, cz), jnp.float32) for t in tiles],
        in_specs=[pl.BlockSpec(memory_space=pltpu.VMEM)] * 2,
        out_specs=[pl.BlockSpec(memory_space=pltpu.VMEM)] * len(tiles),
        compiler_params=pltpu.CompilerParams(vmem_limit_bytes=16 * 2**20),
        name="all_tiles",
    )(potential, orbitals)


def sides_kernel(unit, chunk_groups, rider, cx, cy, *refs):
    low_ref, high_ref = refs[-2:]
    start, groups, first, late = unit
    at = 0
    for g in range(start, start + groups):
        for plane, rows in halo_planes(cx, late):
            which, x = split_plane(plane, cx)
            base = g * cx * cy + x * cy
            low_ref[at : at + rows] = refs[which][base : base + rows]
            high_ref[at : at + rows] = refs[which][base + cy - rows : base + cy]
            at += rows
    if first:
        per = cy // 8
        for plane in diag_planes(cx):
            which, x = split_plane(plane, cx)
            base = chunk_groups * cx * cy + x * per
            low_ref[at] = refs[which][base]
            high_ref[at] = refs[which][base + per - 1]
            at += 1
    if rider is not None:
        for g in range(rider[0], rider[0] + rider[1]):
            for x in range(cx):
                base = g * cx * cy + x * cy
                low_ref[at : at + HALO] = refs[3][base : base + HALO]
                high_ref[at : at + HALO] = refs[3][base + cy - HALO : base + cy]
                at += HALO


def unit_tiles(cx, unit):
    _, groups, first, late = unit
    return groups * sum(rows for _, rows in halo_planes(cx, late)) + (len(diag_planes(cx)) if first else 0)


def pack_sides(blocks, unit, chunk_groups, cx, cy, rider, rider_mid):
    tiles = unit_tiles(cx, unit) + (0 if rider is None else rider[1] * cx * HALO)
    shape = jax.ShapeDtypeStruct((tiles,) + blocks[0].shape[1:], jnp.float32)
    operands = blocks + (() if rider is None else (rider_mid,))
    return pl.pallas_call(
        functools.partial(sides_kernel, unit, chunk_groups, rider, cx, cy),
        out_shape=(shape, shape),
        in_specs=[pl.BlockSpec(memory_space=pltpu.VMEM)] * len(operands),
        out_specs=(pl.BlockSpec(memory_space=pltpu.VMEM),) * 2,
        compiler_params=pltpu.CompilerParams(vmem_limit_bytes=16 * 2**20),
        cost_estimate=pl.CostEstimate(flops=0, bytes_accessed=1_000_000, transcendentals=0),
        name="pack_sides",
    )(*operands)


def z_circulant(cz):
    row = lax.broadcasted_iota(jnp.int32, (cz, cz), 0)
    col = lax.broadcasted_iota(jnp.int32, (cz, cz), 1)
    gap = jnp.where(row >= col, row - col, row - col + cz)
    near = (gap == 1) | (gap == cz - 1)
    far = (gap == 2) | (gap == cz - 2)
    return jnp.where(near, -16.0, jnp.where(far, 1.0, 0.0)).astype(jnp.bfloat16)


def z_part(center, matrix):
    flat = center.reshape(-1, center.shape[-1])
    high = flat.astype(jnp.bfloat16)
    rest = flat - high.astype(jnp.float32)
    middle = rest.astype(jnp.bfloat16)
    low = (rest - middle.astype(jnp.float32)).astype(jnp.bfloat16)

    def times(part):
        return jnp.dot(part, matrix, preferred_element_type=jnp.float32)

    return (times(high) + (times(middle) + times(low))).reshape(center.shape)


def four_steps(cx, cy, chain, diag_ref, out_ref):
    total = cx + 2 * HALO
    matrix = z_circulant(out_ref.shape[-1])
    for step in range(DEG):
        source = chain[step]
        left = HALO - 2 * (step + 1)
        for plane in range(total):
            rows = reach(plane, cx, left)
            if rows < 0:
                continue
            first, count = HALO - rows, cy + 2 * rows
            here = slice(first, first + count)
            column = source[plane, first - 2 : first + count + 2]
            center = column[2:-2]
            near = (column[1:-3] + column[3:-1]) + (source[plane - 1, here] + source[plane + 1, here])
            far = (column[:-4] + column[4:]) + (source[plane - 2, here] + source[plane + 2, here])
            applied = diag_ref[plane, here][:, None, :] * center + FAR * ((z_part(center, matrix) + far) - 16.0 * near)
            fresh = 0.5 * applied if step == 0 else applied - chain[step - 1][plane, here]
            if step < DEG - 1:
                chain[step + 1][plane, here] = fresh
            else:
                out_ref[:, plane - HALO] = jnp.swapaxes(fresh, 0, 1)


def fill_blocks(cx, cy, base, sources, ext_ref):
    for x in range(cx):
        for which in range(3):
            ext_ref[which * cx + x, HALO : HALO + cy] = sources[which][pl.ds(base + x * cy, cy)]


def filter_kernel(unit, chunk_groups, own_at, cx, cy, lo_ref, mid_ref, hi_ref, yl_ref, yh_ref, *refs):
    start, groups, first, late = unit
    group = pl.program_id(0)
    sources = (lo_ref, mid_ref, hi_ref)
    planes = halo_planes(cx, late)
    side = sum(rows for _, rows in planes)
    if first:
        out_ref, diag_ref = refs[:2]

        @pl.when(group == 0)
        def _():
            per = cy // 8
            cz = out_ref.shape[-1]
            for x in range(cx):
                for which in range(3):
                    base = chunk_groups * cx * cy + x * per
                    block = sources[which][base : base + per].reshape(cy, cz)
                    diag_ref[which * cx + x, HALO : HALO + cy] = DIAG_SCALE * block + DIAG_SHIFT
            at = groups * side
            for plane in diag_planes(cx):
                diag_ref[plane, 0:HALO] = DIAG_SCALE * yl_ref[at] + DIAG_SHIFT
                diag_ref[plane, HALO + cy :] = DIAG_SCALE * yh_ref[at] + DIAG_SHIFT
                at += 1
    else:
        diag_ref, out_ref = refs[-6:-4]
    chain = refs[-4:]
    if late:
        for x in range(cx):
            base = own_at + group * cx * HALO + x * HALO
            chain[0][HALO + x, 0:HALO] = refs[0][pl.ds(base, HALO)]
            chain[0][HALO + x, HALO + cy :] = refs[1][pl.ds(base, HALO)]
    for x in range(cx):
        for which in range(3):
            tiles = sources[which][pl.ds((start + group) * cx * cy + x * cy, cy)]
            chain[0][which * cx + x, HALO : HALO + cy] = tiles
    at = 0
    for plane, rows in planes:
        chain[0][plane, HALO - rows : HALO] = yl_ref[pl.ds(group * side + at, rows)]
        chain[0][plane, HALO + cy : HALO + cy + rows] = yh_ref[pl.ds(group * side + at, rows)]
        at += rows
    four_steps(cx, cy, chain, diag_ref, out_ref)


def run_filter(blocks, sides, unit, chunk_groups, own, own_at, cx, cy, cz, diag):
    _, groups, first, late = unit
    ext = (cx + 2 * HALO, cy + 2 * HALO, GROUP, cz)
    out_shape = [jax.ShapeDtypeStruct((groups * GROUP, cx, cy, cz), jnp.float32)]
    out_specs = [pl.BlockSpec((GROUP, cx, cy, cz), lambda g: (g, 0, 0, 0))]
    operands = blocks + sides + (own if late else ())
    if first:
        wide = (cx + 2 * HALO, cy + 2 * HALO, cz)
        out_shape.append(jax.ShapeDtypeStruct(wide, jnp.float32))
        out_specs.append(pl.BlockSpec(wide, lambda g: (0, 0, 0)))
    else:
        operands = operands + (diag,)
    got = pl.pallas_call(
        functools.partial(filter_kernel, unit, chunk_groups, own_at, cx, cy),
        grid=(groups,),
        out_shape=out_shape,
        in_specs=[pl.BlockSpec(memory_space=pltpu.VMEM)] * len(operands),
        out_specs=out_specs,
        scratch_shapes=[pltpu.VMEM(ext, jnp.float32)] * 4,
        compiler_params=pltpu.CompilerParams(vmem_limit_bytes=32 * 2**20),
        cost_estimate=pl.CostEstimate(flops=0, bytes_accessed=groups * FILTER_COST, transcendentals=0),
        name="filter_orbitals",
    )(*operands)
    return got if first else (got[0], diag)


def gram_kernel(offset, scale, counts, *refs):
    chunks, earlier, out_ref, rows_ref = refs[: len(counts)], refs[len(counts) : -2], refs[-2], refs[-1]
    own = chunks[-1]
    count, cx, cy, cz = own.shape
    norb = rows_ref.shape[1]
    rows = []
    for ref, size in zip(chunks, counts):
        for at in range(size):
            rows.append((ref, at))
    rows_ref[...] = jnp.zeros_like(rows_ref)
    block = 4
    for a0 in range(0, count, block):
        a_list = list(range(a0, min(a0 + block, count)))
        last = offset + a_list[-1]
        for j0 in range(0, last + 1, block):
            j_list = list(range(j0, min(j0 + block, last + 1)))
            accs = [None] * (len(a_list) * len(j_list))
            for x in range(cx):
                left = [own[a, x] for a in a_list]
                right = [rows[j][0][rows[j][1], x] for j in j_list]
                at = 0
                for l in left:
                    for r in right:
                        prod = l * r
                        prod = prod[:8] + prod[8:]
                        accs[at] = prod if accs[at] is None else accs[at] + prod
                        at += 1
            at = 0
            for a in a_list:
                for j in j_list:
                    rows_ref[a, j : j + 1, :] = jnp.sum(accs[at], axis=0, keepdims=True)
                    at += 1
    sums = lax.dot_general(
        jnp.ones((8, cz), jnp.float32), rows_ref[...].reshape(count * norb, cz), (((1,), (1,)), ((), ())),
        precision=lax.Precision.HIGHEST, preferred_element_type=jnp.float32,
    )
    lane = lax.broadcasted_iota(jnp.int32, (8, 128), 1)
    row = lax.broadcasted_iota(jnp.int32, (8, 128), 0)
    per = 128 // norb
    packed = jnp.zeros((8, 128), jnp.float32)
    for a in range(count):
        here, slot = a // per, (offset + a) // 8
        value = pltpu.roll(sums[:, 128 * here : 128 * (here + 1)], (norb * (slot - a % per)) % 128, 1)
        mask = (row == (offset + a) % 8) & (lane >= norb * slot) & (lane < norb * (slot + 1))
        packed = packed + jnp.where(mask, value, 0.0)
    packed = packed * scale
    for ref in earlier:
        packed = packed + ref[...]
    out_ref[...] = packed


def run_gram(chunks, earlier, offset, norb, scale):
    count, cx, cy, cz = chunks[-1].shape
    counts = tuple(c.shape[0] for c in chunks)
    operands = tuple(chunks) + tuple(earlier)
    return pl.pallas_call(
        functools.partial(gram_kernel, offset, scale, counts),
        out_shape=jax.ShapeDtypeStruct((8, 128), jnp.float32),
        in_specs=[pl.BlockSpec(memory_space=pltpu.VMEM)] * len(operands),
        out_specs=pl.BlockSpec(memory_space=pltpu.VMEM),
        scratch_shapes=[pltpu.VMEM((count, norb, cz), jnp.float32)],
        compiler_params=pltpu.CompilerParams(vmem_limit_bytes=24 * 2**20),
        cost_estimate=pl.CostEstimate(flops=0, bytes_accessed=100, transcendentals=0),
        name="gram_rows",
    )(*operands)


def factor_table(gram, table_ref):
    norb = gram.shape[0]
    columns = [jnp.broadcast_to(gram[:, j : j + 1], (norb, 128)) for j in range(norb)]
    row = lax.broadcasted_iota(jnp.int32, (norb, 128), 0)
    for k in range(norb):
        scale = 1.0 / jnp.sqrt(columns[k][k : k + 1])
        column = columns[k] * scale
        table_ref[k] = jnp.where(row == k, scale, column)
        for j in range(k + 1, norb):
            top = 8 * (j // 8)
            fresh = columns[j][top:] - column[top:] * column[j : j + 1]
            columns[j] = fresh if top == 0 else jnp.concatenate([jnp.zeros((top, 128), jnp.float32), fresh], axis=0)


def solve_kernel(counts, recv_ref, *refs):
    norb = sum(counts)
    chunks, (out_ref, here_ref, table_ref, sems) = refs[: len(counts)], refs[len(counts) :]
    packed = jnp.sum(recv_ref[...], axis=0)
    rows = jnp.concatenate([packed] + [jnp.roll(packed, -norb * q, 1) for q in range(1, 4)], axis=0)
    factor_table(rows, table_ref)
    where = []
    for ref, count in zip(chunks, counts):
        for at in range(count):
            where.append((ref, at))
    block = 8
    cx = here_ref.shape[1]

    def copy_out(x):
        return pltpu.make_async_copy(here_ref.at[:, x], out_ref.at[:, x], sems.at[x])

    def layer(x, _):
        for i0 in range(0, norb, block):
            accs = [where[i0 + a][0][where[i0 + a][1], x] for a in range(block)]
            for j in range(i0):
                value = here_ref[j, x]
                for a in range(block):
                    accs[a] = accs[a] - table_ref[j, i0 + a : i0 + a + 1, :] * value
            for a in range(block):
                value = accs[a] * table_ref[i0 + a, i0 + a : i0 + a + 1, :]
                here_ref[i0 + a, x] = value
                for c in range(a + 1, block):
                    accs[c] = accs[c] - table_ref[i0 + a, i0 + c : i0 + c + 1, :] * value
        copy_out(x).start()
        return 0

    lax.fori_loop(0, cx, layer, 0)
    for x in range(cx):
        copy_out(x).wait()


def run_solve(received, chunks):
    counts = tuple(c.shape[0] for c in chunks)
    norb = sum(counts)
    _, cx, cy, cz = chunks[0].shape
    return pl.pallas_call(
        functools.partial(solve_kernel, counts),
        out_shape=jax.ShapeDtypeStruct((norb, cx, cy, cz), jnp.float32),
        in_specs=[pl.BlockSpec(memory_space=pltpu.VMEM)] * (1 + len(chunks)),
        out_specs=pl.BlockSpec(memory_space=pl.ANY),
        scratch_shapes=[
            pltpu.VMEM((norb, cx, cy, cz), jnp.float32),
            pltpu.VMEM((norb, norb, 128), jnp.float32),
            pltpu.SemaphoreType.DMA((cx,)),
        ],
        compiler_params=pltpu.CompilerParams(vmem_limit_bytes=24 * 2**20),
        name="orthonormalize",
    )(received, *chunks)


def body(orbitals, potential):
    norb, cx, cy, cz = orbitals.shape
    chips = axis_count(("gx", "gz"))
    scale = 1.0 / float(chips * CORES * cx * cy * cz)
    blocks = []
    first = first_tiles(orbitals, potential)
    for index, mid in enumerate(all_tiles(orbitals, potential)):
        lo, hi = both_ways(*((first, first) if index == 0 else (mid, mid)), "gx")
        blocks.append((lo, mid, hi))
    diag = None
    filtered, grams, all_sides, alone = [], [], [], {}
    for index, (chunk, start, groups) in enumerate(UNITS):
        unit = (start, groups, index == 0, index in RIDES or index in ALONE)
        if index in AFTER:
            lo, mid, hi = blocks[chunk]
            before = AFTER[index]
            tied = (lo, hi, filtered[before]) + ((grams[before],) if before == 0 else ())
            if index in ALONE:
                part = mid[start * cx * cy :][: cx * cy].reshape((cx, cy) + mid.shape[1:])
                rows = [p.reshape((cx * HALO,) + p.shape[2:]) for p in (part[:, :HALO], part[:, cy - HALO :])]
                tied = both_ways(*rows, GY) + tied
            tied = lax.optimization_barrier(tied)
            if index in ALONE:
                alone[index], tied = tied[:2], tied[2:]
            lo, hi, filtered[before], *rest = tied
            grams[before : before + len(rest)] = rest
            blocks[chunk] = lo, mid, hi
        rider, rider_mid = None, None
        for later, carrier in RIDES.items():
            if carrier == index:
                rider, rider_mid = UNITS[later][1:], blocks[UNITS[later][0]][1]
        low, high = pack_sides(blocks[chunk], unit, CHUNKS[chunk], cx, cy, rider, rider_mid)
        all_sides.append(both_ways(low, high, GY))
        own, own_at = None, 0
        if index in RIDES:
            carrier = RIDES[index]
            own = all_sides[carrier]
            own_at = unit_tiles(cx, UNITS[carrier][1:] + (carrier == 0, carrier in RIDES))
        if index in ALONE:
            own = alone[index]
        out, diag = run_filter(blocks[chunk], all_sides[index], unit, CHUNKS[chunk], own, own_at, cx, cy, cz, diag)
        offset = GROUP * sum(g for _, _, g in UNITS[:index])
        filtered.append(out)
        last = index + 1 == len(UNITS)
        grams.append(run_gram(filtered, grams if last else (), offset, norb, scale))
    local = grams[-1]
    other = lax.ppermute(local, "core", [(core, 1 - core) for core in range(CORES)])
    chip = jnp.broadcast_to((local + other)[None], (chips,) + local.shape)
    received = lax.all_to_all(chip, ("gx", "gz"), 0, 0, tiled=True)
    return run_solve(received, filtered)


def solution(mesh):
    count = mesh.shape["gx"], mesh.shape["gy"] // CORES, CORES
    split = jax.sharding.Mesh(mesh.devices.reshape(count), ("gx",) + GY)
    placed = (P(None, "gx", GY, None), P("gx", GY, None))
    return jax.shard_map(
        body, mesh=split, in_specs=placed, out_specs=P(None, "gx", GY, None), check_vma=False
    )
```

profile of v0, /device:TPU:0, one launch (start us, length us, event | category | flops | bytes accessed | tf_op | source)
XLA Modules:
  0.0 96.8 jit_solution(5414378814676688422)
XLA Ops:
  0.0 2.0 %first_tiles.1 = f32[144,8,128]{2,1,0:T(8,128)} custom-call(f32[8,16,128]{2,1,0:T(8,128)} %pot_ref.3, f32[32,8,16,128]{3,2,1,0:T(8,128)} %orb_ref.3), custom_call_target="tpu_custom_call" | custom-call | tf_op jit(solution)/shard_map/first_tiles/pallas_call | solution.py:111
  2.0 1.6 %collective-permute-start.4 = (f32[144,8,128]{2,1,0:T(8,128)}, f32[144,8,128]{2,1,0:T(8,128)S(1)}, u32[]{:S(2)}, u32[]{:S(2)}) collective-permute-start(f32[144,8,128]{2,1,0:T(8,128)} %first_tiles.1), channel_id=1, source_target_pairs={{0,8},{8,16},{16,24},{24,32},{32,40},{40,48},{48,56},{56,64},{64,7... | collective-permute-start | bytes 1769480 | tf_op jit(solution)/shard_map/ppermute | solution.py:43
  3.7 3.8 %collective-permute-start.5 = (f32[144,8,128]{2,1,0:T(8,128)}, f32[144,8,128]{2,1,0:T(8,128)S(1)}, u32[]{:S(2)}, u32[]{:S(2)}) collective-permute-start(f32[144,8,128]{2,1,0:T(8,128)} %first_tiles.1), channel_id=1, source_target_pairs={{0,120},{8,0},{16,8},{24,16},{32,24},{40,32},{48,40},{56,48},{64,5... | collective-permute-start | bytes 1769480 | tf_op jit(solution)/shard_map/ppermute | solution.py:44
  7.5 0.4 all_tiles.1
  7.9 0.1 collective-permute-start.2
  7.9 5.3 %collective-permute-start.3 = (f32[256,8,128]{2,1,0:T(8,128)S(1)}, f32[256,8,128]{2,1,0:T(8,128)S(1)}, u32[]{:S(2)}, u32[]{:S(2)}) collective-permute-start(f32[256,8,128]{2,1,0:T(8,128)S(1)} %get-tuple-element.27.refs_1_.mid_ref), channel_id=1, source_target_pairs={{0,120},{8,0},{16,8},{24,16},{32,24},{40,32},{48,40},{56,48},{64,5... | collective-permute-start | bytes 3145736 | tf_op jit(solution)/shard_map/ppermute | solution.py:44
  13.3 8.5 %collective-permute-done.4.refs_0_.lo_ref = f32[144,8,128]{2,1,0:T(8,128)S(1)} collective-permute-done((f32[144,8,128]{2,1,0:T(8,128)}, f32[144,8,128]{2,1,0:T(8,128)S(1)}, u32[]{:S(2)}, u32[]{:S(2)}) %collective-permute-start.4) | collective-permute-done | bytes 589856 | tf_op jit(solution)/shard_map/ppermute | solution.py:43
  21.8 0.1 pack_sides.4
  21.9 0.0 collective-permute-start.6
  22.0 3.0 %collective-permute-start.7 = (f32[128,8,128]{2,1,0:T(8,128)S(1)}, f32[128,8,128]{2,1,0:T(8,128)S(1)}, u32[]{:S(2)}, u32[]{:S(2)}) collective-permute-start(f32[128,8,128]{2,1,0:T(8,128)S(1)} %get-tuple-element.30), channel_id=1, source_target_pairs={{0,7},{1,0},{2,1},{3,2},{4,3},{5,4},{6,5},{7,6},{8,15},{9,8},{10,9... | collective-permute-start | bytes 1572872 | tf_op jit(solution)/shard_map/ppermute | solution.py:44
  25.0 9.5 %collective-permute-done.refs_0_ = f32[64,8,128]{2,1,0:T(8,128)S(1)} collective-permute-done((f32[64,8,128]{2,1,0:T(8,128)S(1)}, f32[64,8,128]{2,1,0:T(8,128)S(1)}, u32[]{:S(2)}, u32[]{:S(2)}) %collective-permute-start) | collective-permute-done | bytes 262176 | tf_op jit(solution)/shard_map/ppermute | solution.py:43
  34.5 5.4 %collective-permute-start.9 = (f32[128,8,128]{2,1,0:T(8,128)S(1)}, f32[128,8,128]{2,1,0:T(8,128)S(1)}, u32[]{:S(2)}, u32[]{:S(2)}) collective-permute-start(f32[128,8,128]{2,1,0:T(8,128)S(1)} %get-tuple-element.33.refs_1_.mid_ref), channel_id=1, source_target_pairs={{0,120},{8,0},{16,8},{24,16},{32,24},{40,32},{48,40},{56,48},{64,5... | collective-permute-start | bytes 1572872 | tf_op jit(solution)/shard_map/ppermute | solution.py:44
  39.9 4.4 %filter_orbitals.4 = (f32[8,8,16,128]{3,2,1,0:T(8,128)S(1)}, f32[24,32,128]{2,1,0:T(8,128)S(1)}) custom-call(f32[144,8,128]{2,1,0:T(8,128)S(1)} %collective-permute-done.4.refs_0_.lo_ref, f32[144,8,128]{2,1,0:T(8,128)S(1)} %get-tuple-element.28.refs_1_.mid_ref, f32[144,8,128]{2,1,0:T(8,128)S(1)} %collective-permute-done.5.refs_2_.hi_ref, ...), custom_call_target="tpu_custom_call" | custom-call | bytes 100 | tf_op jit(solution)/shard_map/filter_orbitals/pallas_call | solution.py:308
  44.3 0.5 gram_rows.4.refs_4_
  44.8 0.0 collective-permute-done.1.refs_1_
  44.9 0.5 collective-permute-start.10
  45.4 2.5 %collective-permute-start.11 = (f32[48,8,128]{2,1,0:T(8,128)S(1)}, f32[48,8,128]{2,1,0:T(8,128)S(1)}, u32[]{:S(2)}, u32[]{:S(2)}) collective-permute-start(f32[48,8,128]{2,1,0:T(8,128)S(1)} %get-tuple-element.37), channel_id=1, source_target_pairs={{0,7},{1,0},{2,1},{3,2},{4,3},{5,4},{6,5},{7,6},{8,15},{9,8},{10,9... | collective-permute-start | bytes 589832 | tf_op jit(solution)/shard_map/ppermute | solution.py:44
  47.9 0.1 pack_sides.6
  48.0 3.2 %collective-permute-done.10.yl_ref = f32[48,8,128]{2,1,0:T(8,128)S(1)} collective-permute-done((f32[48,8,128]{2,1,0:T(8,128)S(1)}, f32[48,8,128]{2,1,0:T(8,128)S(1)}, u32[]{:S(2)}, u32[]{:S(2)}) %collective-permute-start.10) | collective-permute-done | bytes 196640 | tf_op jit(solution)/shard_map/ppermute | solution.py:43
  51.2 4.3 %filter_orbitals.5.refs_1_ = f32[8,8,16,128]{3,2,1,0:T(8,128)S(1)} custom-call(f32[256,8,128]{2,1,0:T(8,128)S(1)} %collective-permute-done.2.refs_0_.lo_ref, f32[256,8,128]{2,1,0:T(8,128)S(1)} %get-tuple-element.27.refs_1_.mid_ref, f32[256,8,128]{2,1,0:T(8,128)S(1)} %collective-permute-done.3.refs_2_.hi_ref, ...), custom_call_target="tpu_custom_call" | custom-call | bytes 100 | tf_op jit(solution)/shard_map/filter_orbitals/pallas_call | solution.py:308
  55.6 0.1 pack_sides.7
  55.7 0.6 collective-permute-start.14
  56.3 2.7 %collective-permute-start.15 = (f32[112,8,128]{2,1,0:T(8,128)S(1)}, f32[112,8,128]{2,1,0:T(8,128)S(1)}, u32[]{:S(2)}, u32[]{:S(2)}) collective-permute-start(f32[112,8,128]{2,1,0:T(8,128)S(1)} %get-tuple-element.47), channel_id=1, source_target_pairs={{0,7},{1,0},{2,1},{3,2},{4,3},{5,4},{6,5},{7,6},{8,15},{9,8},{10,9... | collective-permute-start | bytes 1376264 | tf_op jit(solution)/shard_map/ppermute | solution.py:44
  59.0 0.8 gram_rows.5.refs_5_
  59.8 4.5 %filter_orbitals.6.refs_2_ = f32[8,8,16,128]{3,2,1,0:T(8,128)S(1)} custom-call(f32[256,8,128]{2,1,0:T(8,128)S(1)} %collective-permute-done.2.refs_0_.lo_ref, f32[256,8,128]{2,1,0:T(8,128)S(1)} %get-tuple-element.27.refs_1_.mid_ref, f32[256,8,128]{2,1,0:T(8,128)S(1)} %collective-permute-done.3.refs_2_.hi_ref, ...), custom_call_target="tpu_custom_call" | custom-call | bytes 100 | tf_op jit(solution)/shard_map/filter_orbitals/pallas_call | solution.py:308
  64.3 1.1 %gram_rows.6.refs_6_ = f32[8,128]{1,0:T(8,128)S(1)} custom-call(f32[8,8,16,128]{3,2,1,0:T(8,128)S(1)} %get-tuple-element.32.refs_0_, f32[8,8,16,128]{3,2,1,0:T(8,128)S(1)} %filter_orbitals.5.refs_1_, f32[8,8,16,128]{3,2,1,0:T(8,128)S(1)} %filter_orbitals.6.refs_2_), custom_call_target="tpu_custom_call" | custom-call | bytes 100 | tf_op jit(solution)/shard_map/gram_rows/pallas_call | solution.py:377
  65.5 4.3 %filter_orbitals.7.refs_3_ = f32[8,8,16,128]{3,2,1,0:T(8,128)S(1)} custom-call(f32[128,8,128]{2,1,0:T(8,128)S(1)} %collective-permute-done.8.refs_0_.lo_ref, f32[128,8,128]{2,1,0:T(8,128)S(1)} %get-tuple-element.33.refs_1_.mid_ref, f32[128,8,128]{2,1,0:T(8,128)S(1)} %collective-permute-done.9.refs_2_.hi_ref, ...), custom_call_target="tpu_custom_call" | custom-call | bytes 100 | tf_op jit(solution)/shard_map/filter_orbitals/pallas_call | solution.py:308
  69.8 1.4 %gram_rows.7 = f32[8,128]{1,0:T(8,128)S(1)} custom-call(f32[8,8,16,128]{3,2,1,0:T(8,128)S(1)} %get-tuple-element.32.refs_0_, f32[8,8,16,128]{3,2,1,0:T(8,128)S(1)} %filter_orbitals.5.refs_1_, f32[8,8,16,128]{3,2,1,0:T(8,128)S(1)} %filter_orbitals.6.refs_2_, f32[8,8,16,128]{3,2,1,0:T(8,128)S(1)} %filter_orbitals.7.refs_3_, f32[8,128]{1,0:T(8,128)S(1)} %gram_rows.4.refs_4_, ...), custom_call_target="tpu_custom_call" | custom-call | bytes 100 | tf_op jit(solution)/shard_map/gram_rows/pallas_call | solution.py:377
  71.3 0.1 collective-permute-start.16
  71.3 1.2 %collective-permute-done.16 = f32[8,128]{1,0:T(8,128)S(1)} collective-permute-done((f32[8,128]{1,0:T(8,128)S(1)}, f32[8,128]{1,0:T(8,128)S(1)}, u32[]{:S(2)}, u32[]{:S(2)}) %collective-permute-start.16) | collective-permute-done | bytes 4128 | tf_op jit(solution)/shard_map/ppermute | solution.py:504
  72.5 20.2 %all_to_all.5.recv_ref = f32[64,8,128]{2,1,0:T(8,128)S(1)} all-to-all(f32[64,8,128]{2,1,0:T(8,128)S(1)} %broadcast_in_dim.2), channel_id=1, replica_groups=mesh['gx'=16,'gz'=4,'core'=2] {'gx','gz'}, dimensions={0} | all-to-all | bytes 524288 | tf_op jit(solution)/shard_map/all_to_all | solution.py:506
  92.7 3.9 %orthonormalize.1 = f32[32,8,16,128]{3,2,1,0:T(8,128)} custom-call(f32[64,8,128]{2,1,0:T(8,128)S(1)} %all_to_all.5.recv_ref, f32[8,8,16,128]{3,2,1,0:T(8,128)S(1)} %get-tuple-element.32.refs_0_, f32[8,8,16,128]{3,2,1,0:T(8,128)S(1)} %filter_orbitals.5.refs_1_, f32[8,8,16,128]{3,2,1,0:T(8,128)S(1)} %filter_orbitals.6.refs_2_, ...), custom_call_target="tpu_custom_call" | custom-call | tf_op jit(solution)/shard_map/orthonormalize/pallas_call | solution.py:443
  (26 shorter events, 0.2 us)
Async XLA Ops:
  0.0 7.5 %copy-start = (f32[32,8,16,128]{3,2,1,0:T(8,128)S(1)}, f32[32,8,16,128]{3,2,1,0:T(8,128)}, u32[]{:S(2)}) copy-start(f32[32,8,16,128]{3,2,1,0:T(8,128)} %orb_ref.3) | copy-start | bytes 6291460
  0.0 7.5 %copy-start.1 = (f32[8,16,128]{2,1,0:T(8,128)S(1)}, f32[8,16,128]{2,1,0:T(8,128)}, u32[]{:S(2)}) copy-start(f32[8,16,128]{2,1,0:T(8,128)} %pot_ref.3) | copy-start | bytes 196612
  2.0 19.8 %collective-permute-start.4 = (f32[144,8,128]{2,1,0:T(8,128)}, f32[144,8,128]{2,1,0:T(8,128)S(1)}, u32[]{:S(2)}, u32[]{:S(2)}) collective-permute-start(f32[144,8,128]{2,1,0:T(8,128)} %first_tiles.1), channel_id=1, source_target_pairs={{0,8},{8,16},{16,24},{24,32},{32,40},{40,48},{48,56},{56,64},{64,7... | collective-permute-start | bytes 1769480 | tf_op jit(solution)/shard_map/ppermute | solution.py:43
  3.7 18.1 %collective-permute-start.5 = (f32[144,8,128]{2,1,0:T(8,128)}, f32[144,8,128]{2,1,0:T(8,128)S(1)}, u32[]{:S(2)}, u32[]{:S(2)}) collective-permute-start(f32[144,8,128]{2,1,0:T(8,128)} %first_tiles.1), channel_id=1, source_target_pairs={{0,120},{8,0},{16,8},{24,16},{32,24},{40,32},{48,40},{56,48},{64,5... | collective-permute-start | bytes 1769480 | tf_op jit(solution)/shard_map/ppermute | solution.py:44
  7.9 36.9 %collective-permute-start.2 = (f32[256,8,128]{2,1,0:T(8,128)S(1)}, f32[256,8,128]{2,1,0:T(8,128)S(1)}, u32[]{:S(2)}, u32[]{:S(2)}) collective-permute-start(f32[256,8,128]{2,1,0:T(8,128)S(1)} %get-tuple-element.27.refs_1_.mid_ref), channel_id=1, source_target_pairs={{0,8},{8,16},{16,24},{24,32},{32,40},{40,48},{48,56},{56,64},{64,7... | collective-permute-start | bytes 3145736 | tf_op jit(solution)/shard_map/ppermute | solution.py:43
  7.9 36.9 %collective-permute-start.3 = (f32[256,8,128]{2,1,0:T(8,128)S(1)}, f32[256,8,128]{2,1,0:T(8,128)S(1)}, u32[]{:S(2)}, u32[]{:S(2)}) collective-permute-start(f32[256,8,128]{2,1,0:T(8,128)S(1)} %get-tuple-element.27.refs_1_.mid_ref), channel_id=1, source_target_pairs={{0,120},{8,0},{16,8},{24,16},{32,24},{40,32},{48,40},{56,48},{64,5... | collective-permute-start | bytes 3145736 | tf_op jit(solution)/shard_map/ppermute | solution.py:44
  21.9 12.6 %collective-permute-start.6 = (f32[128,8,128]{2,1,0:T(8,128)S(1)}, f32[128,8,128]{2,1,0:T(8,128)S(1)}, u32[]{:S(2)}, u32[]{:S(2)}) collective-permute-start(f32[128,8,128]{2,1,0:T(8,128)S(1)} %get-tuple-element.29), channel_id=1, source_target_pairs={{0,1},{1,2},{2,3},{3,4},{4,5},{5,6},{6,7},{7,0},{8,9},{9,10},{10,1... | collective-permute-start | bytes 1572872 | tf_op jit(solution)/shard_map/ppermute | solution.py:43
  22.0 18.0 %collective-permute-start.7 = (f32[128,8,128]{2,1,0:T(8,128)S(1)}, f32[128,8,128]{2,1,0:T(8,128)S(1)}, u32[]{:S(2)}, u32[]{:S(2)}) collective-permute-start(f32[128,8,128]{2,1,0:T(8,128)S(1)} %get-tuple-element.30), channel_id=1, source_target_pairs={{0,7},{1,0},{2,1},{3,2},{4,3},{5,4},{6,5},{7,6},{8,15},{9,8},{10,9... | collective-permute-start | bytes 1572872 | tf_op jit(solution)/shard_map/ppermute | solution.py:44
  25.0 9.6 %collective-permute-start = (f32[64,8,128]{2,1,0:T(8,128)S(1)}, f32[64,8,128]{2,1,0:T(8,128)S(1)}, u32[]{:S(2)}, u32[]{:S(2)}) collective-permute-start(f32[64,8,128]{2,1,0:T(8,128)S(1)} %bitcast.5), channel_id=1, source_target_pairs={{0,1},{1,2},{2,3},{3,4},{4,5},{5,6},{6,7},{7,0},{8,9},{9,10},{10,1... | collective-permute-start | bytes 786440 | tf_op jit(solution)/shard_map/ppermute | solution.py:43
  34.5 21.1 %collective-permute-start.8 = (f32[128,8,128]{2,1,0:T(8,128)S(1)}, f32[128,8,128]{2,1,0:T(8,128)S(1)}, u32[]{:S(2)}, u32[]{:S(2)}) collective-permute-start(f32[128,8,128]{2,1,0:T(8,128)S(1)} %get-tuple-element.33.refs_1_.mid_ref), channel_id=1, source_target_pairs={{0,8},{8,16},{16,24},{24,32},{32,40},{40,48},{48,56},{56,64},{64,7... | collective-permute-start | bytes 1572872 | tf_op jit(solution)/shard_map/ppermute | solution.py:43
  34.5 21.1 %collective-permute-start.9 = (f32[128,8,128]{2,1,0:T(8,128)S(1)}, f32[128,8,128]{2,1,0:T(8,128)S(1)}, u32[]{:S(2)}, u32[]{:S(2)}) collective-permute-start(f32[128,8,128]{2,1,0:T(8,128)S(1)} %get-tuple-element.33.refs_1_.mid_ref), channel_id=1, source_target_pairs={{0,120},{8,0},{16,8},{24,16},{32,24},{40,32},{48,40},{56,48},{64,5... | collective-permute-start | bytes 1572872 | tf_op jit(solution)/shard_map/ppermute | solution.py:44
  39.9 4.8 %collective-permute-start.1 = (f32[64,8,128]{2,1,0:T(8,128)S(1)}, f32[64,8,128]{2,1,0:T(8,128)S(1)}, u32[]{:S(2)}, u32[]{:S(2)}) collective-permute-start(f32[64,8,128]{2,1,0:T(8,128)S(1)} %bitcast.4), channel_id=1, source_target_pairs={{0,7},{1,0},{2,1},{3,2},{4,3},{5,4},{6,5},{7,6},{8,15},{9,8},{10,9... | collective-permute-start | bytes 786440 | tf_op jit(solution)/shard_map/ppermute | solution.py:44
  44.9 6.4 %collective-permute-start.10 = (f32[48,8,128]{2,1,0:T(8,128)S(1)}, f32[48,8,128]{2,1,0:T(8,128)S(1)}, u32[]{:S(2)}, u32[]{:S(2)}) collective-permute-start(f32[48,8,128]{2,1,0:T(8,128)S(1)} %get-tuple-element.36), channel_id=1, source_target_pairs={{0,1},{1,2},{2,3},{3,4},{4,5},{5,6},{6,7},{7,0},{8,9},{9,10},{10,1... | collective-permute-start | bytes 589832 | tf_op jit(solution)/shard_map/ppermute | solution.py:43
  45.4 5.9 %collective-permute-start.11 = (f32[48,8,128]{2,1,0:T(8,128)S(1)}, f32[48,8,128]{2,1,0:T(8,128)S(1)}, u32[]{:S(2)}, u32[]{:S(2)}) collective-permute-start(f32[48,8,128]{2,1,0:T(8,128)S(1)} %get-tuple-element.37), channel_id=1, source_target_pairs={{0,7},{1,0},{2,1},{3,2},{4,3},{5,4},{6,5},{7,6},{8,15},{9,8},{10,9... | collective-permute-start | bytes 589832 | tf_op jit(solution)/shard_map/ppermute | solution.py:44
  48.0 11.8 %collective-permute-start.12 = (f32[112,8,128]{2,1,0:T(8,128)S(1)}, f32[112,8,128]{2,1,0:T(8,128)S(1)}, u32[]{:S(2)}, u32[]{:S(2)}) collective-permute-start(f32[112,8,128]{2,1,0:T(8,128)S(1)} %get-tuple-element.42), channel_id=1, source_target_pairs={{0,1},{1,2},{2,3},{3,4},{4,5},{5,6},{6,7},{7,0},{8,9},{9,10},{10,1... | collective-permute-start | bytes 1376264 | tf_op jit(solution)/shard_map/ppermute | solution.py:43
  51.2 8.6 %collective-permute-start.13 = (f32[112,8,128]{2,1,0:T(8,128)S(1)}, f32[112,8,128]{2,1,0:T(8,128)S(1)}, u32[]{:S(2)}, u32[]{:S(2)}) collective-permute-start(f32[112,8,128]{2,1,0:T(8,128)S(1)} %get-tuple-element.43), channel_id=1, source_target_pairs={{0,7},{1,0},{2,1},{3,2},{4,3},{5,4},{6,5},{7,6},{8,15},{9,8},{10,9... | collective-permute-start | bytes 1376264 | tf_op jit(solution)/shard_map/ppermute | solution.py:44
  55.7 9.8 %collective-permute-start.14 = (f32[112,8,128]{2,1,0:T(8,128)S(1)}, f32[112,8,128]{2,1,0:T(8,128)S(1)}, u32[]{:S(2)}, u32[]{:S(2)}) collective-permute-start(f32[112,8,128]{2,1,0:T(8,128)S(1)} %get-tuple-element.46), channel_id=1, source_target_pairs={{0,1},{1,2},{2,3},{3,4},{4,5},{5,6},{6,7},{7,0},{8,9},{9,10},{10,1... | collective-permute-start | bytes 1376264 | tf_op jit(solution)/shard_map/ppermute | solution.py:43
  56.3 9.2 %collective-permute-start.15 = (f32[112,8,128]{2,1,0:T(8,128)S(1)}, f32[112,8,128]{2,1,0:T(8,128)S(1)}, u32[]{:S(2)}, u32[]{:S(2)}) collective-permute-start(f32[112,8,128]{2,1,0:T(8,128)S(1)} %get-tuple-element.47), channel_id=1, source_target_pairs={{0,7},{1,0},{2,1},{3,2},{4,3},{5,4},{6,5},{7,6},{8,15},{9,8},{10,9... | collective-permute-start | bytes 1376264 | tf_op jit(solution)/shard_map/ppermute | solution.py:44
  71.3 1.2 %collective-permute-start.16 = (f32[8,128]{1,0:T(8,128)S(1)}, f32[8,128]{1,0:T(8,128)S(1)}, u32[]{:S(2)}, u32[]{:S(2)}) collective-permute-start(f32[8,128]{1,0:T(8,128)S(1)} %gram_rows.7), channel_id=1, source_target_pairs={{0,1},{1,0},{2,3},{3,2},{4,5},{5,4},{6,7},{7,6},{8,9},{9,8},{10,11... | collective-permute-start | bytes 12296 | tf_op jit(solution)/shard_map/ppermute | solution.py:504
where the time goes:
time: 96.9 us; the launch traced here: 96.8 us
  Pallas kernels  27.8 us (29%)
  starting transfers between devices  25.7 us (27%)
  waiting for transfers between devices  22.5 us (23%)
  blocking collectives  20.2 us (21%)
    ppermute x8, starting transfers between devices, both_ways(): lax.ppermute(low_part, axis, shift_perm(axis, -1))  22.7 us
    ppermute x8, waiting for transfers between devices, both_ways(): lax.ppermute(high_part, axis, shift_perm(axis, 1))  21.3 us
    all_to_all x1, blocking collectives, body(): received = lax.all_to_all(chip, ('gx', 'gz'), 0, 0, tiled=True)  20.2 us
    pallas_call x4, Pallas kernels, run_filter(): pl.pallas_call(functools.partial(filter_kernel, unit, chunk_groups, own_a...  17.6 us
    pallas_call x1, Pallas kernels, run_solve(): pl.pallas_call(functools.partial(solve_kernel, counts), out_shape=jax.Sha...  3.87 us
    pallas_call x4, Pallas kernels, run_gram(): pl.pallas_call(functools.partial(gram_kernel, offset, scale, counts), out...  3.74 us
    ppermute x8, starting transfers between devices, both_ways(): lax.ppermute(high_part, axis, shift_perm(axis, 1))  2.93 us
    pallas_call x1, Pallas kernels, first_tiles(): pl.pallas_call(functools.partial(first_tiles_kernel, groups, pieces), out...  2.02 us
  transfers between devices with their start and end apart: 17, of which 4 were waited for; matrix products, arithmetic and copies ran while one was open for 0% of the time, Pallas kernels for 17%

commit v1 on v0

--- a/solution.py
+++ b/solution.py
@@ -220,9 +220,14 @@
     return (times(high) + (times(middle) + times(low))).reshape(center.shape)
 
 
-def four_steps(cx, cy, chain, diag_ref, out_ref):
+def four_steps(cx, cy, start, steps, diag_ref, out_ref):
     total = cx + 2 * HALO
     matrix = z_circulant(out_ref.shape[-1])
+
+    def rows_of(ref):
+        return lambda plane, a, b: ref[plane, a:b]
+
+    chain = [start] + [rows_of(ref) for ref in steps]
     for step in range(DEG):
         source = chain[step]
         left = HALO - 2 * (step + 1)
@@ -230,90 +235,81 @@
             rows = reach(plane, cx, left)
             if rows < 0:
                 continue
-            first, count = HALO - rows, cy + 2 * rows
-            here = slice(first, first + count)
-            column = source[plane, first - 2 : first + count + 2]
+            first, last = HALO - rows, HALO + cy + rows
+            column = source(plane, first - 2, last + 2)
             center = column[2:-2]
-            near = (column[1:-3] + column[3:-1]) + (source[plane - 1, here] + source[plane + 1, here])
-            far = (column[:-4] + column[4:]) + (source[plane - 2, here] + source[plane + 2, here])
-            applied = diag_ref[plane, here][:, None, :] * center + FAR * ((z_part(center, matrix) + far) - 16.0 * near)
-            fresh = 0.5 * applied if step == 0 else applied - chain[step - 1][plane, here]
+            near = (column[1:-3] + column[3:-1]) + (source(plane - 1, first, last) + source(plane + 1, first, last))
+            far = (column[:-4] + column[4:]) + (source(plane - 2, first, last) + source(plane + 2, first, last))
+            diag = diag_ref[plane, first:last][:, None, :]
+            applied = diag * center + FAR * ((z_part(center, matrix) + far) - 16.0 * near)
+            fresh = 0.5 * applied if step == 0 else applied - chain[step - 1](plane, first, last)
             if step < DEG - 1:
-                chain[step + 1][plane, here] = fresh
+                steps[step][plane, first:last] = fresh
             else:
                 out_ref[:, plane - HALO] = jnp.swapaxes(fresh, 0, 1)
 
 
-def fill_blocks(cx, cy, base, sources, ext_ref):
-    for x in range(cx):
-        for which in range(3):
-            ext_ref[which * cx + x, HALO : HALO + cy] = sources[which][pl.ds(base + x * cy, cy)]
-
-
 def filter_kernel(unit, chunk_groups, own_at, cx, cy, lo_ref, mid_ref, hi_ref, yl_ref, yh_ref, *refs):
     start, groups, first, late = unit
-    group = pl.program_id(0)
     sources = (lo_ref, mid_ref, hi_ref)
     planes = halo_planes(cx, late)
-    side = sum(rows for _, rows in planes)
+    sides = {}
+    at = 0
+    for plane, rows in planes:
+        sides[plane] = (yl_ref, yh_ref, at, rows)
+        at += rows
+    if late:
+        for x in range(cx):
+            sides[HALO + x] = (refs[0], refs[1], own_at + x * HALO, HALO)
     if first:
         out_ref, diag_ref = refs[:2]
-
-        @pl.when(group == 0)
-        def _():
-            per = cy // 8
-            cz = out_ref.shape[-1]
-            for x in range(cx):
-                for which in range(3):
-                    base = chunk_groups * cx * cy + x * per
-                    block = sources[which][base : base + per].reshape(cy, cz)
-                    diag_ref[which * cx + x, HALO : HALO + cy] = DIAG_SCALE * block + DIAG_SHIFT
-            at = groups * side
-            for plane in diag_planes(cx):
-                diag_ref[plane, 0:HALO] = DIAG_SCALE * yl_ref[at] + DIAG_SHIFT
-                diag_ref[plane, HALO + cy :] = DIAG_SCALE * yh_ref[at] + DIAG_SHIFT
-                at += 1
+        per = cy // 8
+        cz = out_ref.shape[-1]
+        for x in range(cx):
+            for which in range(3):
+                base = chunk_groups * cx * cy + x * per
+                block = sources[which][base : base + per].reshape(cy, cz)
+                diag_ref[which * cx + x, HALO : HALO + cy] = DIAG_SCALE * block + DIAG_SHIFT
+        for plane in diag_planes(cx):
+            diag_ref[plane, 0:HALO] = DIAG_SCALE * yl_ref[at] + DIAG_SHIFT
+            diag_ref[plane, HALO + cy :] = DIAG_SCALE * yh_ref[at] + DIAG_SHIFT
+            at += 1
     else:
-        diag_ref, out_ref = refs[-6:-4]
-    chain = refs[-4:]
-    if late:
-        for x in range(cx):
-            base = own_at + group * cx * HALO + x * HALO
-            chain[0][HALO + x, 0:HALO] = refs[0][pl.ds(base, HALO)]
-            chain[0][HALO + x, HALO + cy :] = refs[1][pl.ds(base, HALO)]
-    for x in range(cx):
-        for which in range(3):
-            tiles = sources[which][pl.ds((start + group) * cx * cy + x * cy, cy)]
-            chain[0][which * cx + x, HALO : HALO + cy] = tiles
-    at = 0
-    for plane, rows in planes:
-        chain[0][plane, HALO - rows : HALO] = yl_ref[pl.ds(group * side + at, rows)]
-        chain[0][plane, HALO + cy : HALO + cy + rows] = yh_ref[pl.ds(group * side + at, rows)]
-        at += rows
-    four_steps(cx, cy, chain, diag_ref, out_ref)
+        diag_ref, out_ref = refs[-5:-3]
+
+    def rows_of(plane, a, b):
+        which, x = split_plane(plane, cx)
+        base = (start * cx + x) * cy - HALO
+        parts = [sources[which][base + max(a, HALO) : base + min(b, HALO + cy)]]
+        if a < HALO:
+            low, _, at, rows = sides[plane]
+            parts.insert(0, low[at + a - (HALO - rows) : at + rows])
+        if b > HALO + cy:
+            _, high, at, _ = sides[plane]
+            parts.append(high[at : at + b - HALO - cy])
+        return parts[0] if len(parts) == 1 else jnp.concatenate(parts, axis=0)
+
+    four_steps(cx, cy, rows_of, refs[-3:], diag_ref, out_ref)
 
 
 def run_filter(blocks, sides, unit, chunk_groups, own, own_at, cx, cy, cz, diag):
     _, groups, first, late = unit
+    assert groups == 1
     ext = (cx + 2 * HALO, cy + 2 * HALO, GROUP, cz)
-    out_shape = [jax.ShapeDtypeStruct((groups * GROUP, cx, cy, cz), jnp.float32)]
-    out_specs = [pl.BlockSpec((GROUP, cx, cy, cz), lambda g: (g, 0, 0, 0))]
+    out_shape = [jax.ShapeDtypeStruct((GROUP, cx, cy, cz), jnp.float32)]
     operands = blocks + sides + (own if late else ())
     if first:
-        wide = (cx + 2 * HALO, cy + 2 * HALO, cz)
-        out_shape.append(jax.ShapeDtypeStruct(wide, jnp.float32))
-        out_specs.append(pl.BlockSpec(wide, lambda g: (0, 0, 0)))
+        out_shape.append(jax.ShapeDtypeStruct((cx + 2 * HALO, cy + 2 * HALO, cz), jnp.float32))
     else:
         operands = operands + (diag,)
     got = pl.pallas_call(
         functools.partial(filter_kernel, unit, chunk_groups, own_at, cx, cy),
-        grid=(groups,),
         out_shape=out_shape,
         in_specs=[pl.BlockSpec(memory_space=pltpu.VMEM)] * len(operands),
-        out_specs=out_specs,
-        scratch_shapes=[pltpu.VMEM(ext, jnp.float32)] * 4,
+        out_specs=[pl.BlockSpec(memory_space=pltpu.VMEM)] * len(out_shape),
+        scratch_shapes=[pltpu.VMEM(ext, jnp.float32)] * 3,
         compiler_params=pltpu.CompilerParams(vmem_limit_bytes=32 * 2**20),
-        cost_estimate=pl.CostEstimate(flops=0, bytes_accessed=groups * FILTER_COST, transcendentals=0),
+        cost_estimate=pl.CostEstimate(flops=0, bytes_accessed=FILTER_COST, transcendentals=0),
         name="filter_orbitals",
     )(*operands)
     return got if first else (got[0], diag)

time: 96.9 us -> 96.9 us (level)
  no operation moved by 1% of the time
where the time goes in v1:
time: 96.9 us; the launch traced here: 96.7 us
  Pallas kernels  27.8 us (29%)
  starting transfers between devices  25.7 us (27%)
  waiting for transfers between devices  22.5 us (23%)
  blocking collectives  20.2 us (21%)
    ppermute x8, starting transfers between devices, both_ways(): lax.ppermute(low_part, axis, shift_perm(axis, -1))  22.7 us
    ppermute x8, waiting for transfers between devices, both_ways(): lax.ppermute(high_part, axis, shift_perm(axis, 1))  21.3 us
    all_to_all x1, blocking collectives, body(): received = lax.all_to_all(chip, ('gx', 'gz'), 0, 0, tiled=True)  20.2 us
    pallas_call x4, Pallas kernels, run_filter(): pl.pallas_call(functools.partial(filter_kernel, unit, chunk_groups, own_a...  17.6 us
    pallas_call x1, Pallas kernels, run_solve(): pl.pallas_call(functools.partial(solve_kernel, counts), out_shape=jax.Sha...  3.87 us
    pallas_call x4, Pallas kernels, run_gram(): pl.pallas_call(functools.partial(gram_kernel, offset, scale, counts), out...  3.74 us
    ppermute x8, starting transfers between devices, both_ways(): lax.ppermute(high_part, axis, shift_perm(axis, 1))  2.94 us
    pallas_call x1, Pallas kernels, first_tiles(): pl.pallas_call(functools.partial(first_tiles_kernel, groups, pieces), out...  2.02 us
  transfers between devices with their start and end apart: 17, of which 4 were waited for; matrix products, arithmetic and copies ran while one was open for 0% of the time, Pallas kernels for 17%

profile of v1, /device:TPU:0, one launch (start us, length us, event | category | flops | bytes accessed | tf_op | source)
XLA Modules:
  0.0 96.7 jit_solution(16238367412115113826)
XLA Ops:
  0.0 2.0 %first_tiles.1 = f32[144,8,128]{2,1,0:T(8,128)} custom-call(f32[8,16,128]{2,1,0:T(8,128)} %pot_ref.3, f32[32,8,16,128]{3,2,1,0:T(8,128)} %orb_ref.3), custom_call_target="tpu_custom_call" | custom-call | tf_op jit(solution)/shard_map/first_tiles/pallas_call | solution.py:111
  2.0 1.6 %collective-permute-start.4 = (f32[144,8,128]{2,1,0:T(8,128)}, f32[144,8,128]{2,1,0:T(8,128)S(1)}, u32[]{:S(2)}, u32[]{:S(2)}) collective-permute-start(f32[144,8,128]{2,1,0:T(8,128)} %first_tiles.1), channel_id=1, source_target_pairs={{0,8},{8,16},{16,24},{24,32},{32,40},{40,48},{48,56},{56,64},{64,7... | collective-permute-start | bytes 1769480 | tf_op jit(solution)/shard_map/ppermute | solution.py:43
  3.7 3.8 %collective-permute-start.5 = (f32[144,8,128]{2,1,0:T(8,128)}, f32[144,8,128]{2,1,0:T(8,128)S(1)}, u32[]{:S(2)}, u32[]{:S(2)}) collective-permute-start(f32[144,8,128]{2,1,0:T(8,128)} %first_tiles.1), channel_id=1, source_target_pairs={{0,120},{8,0},{16,8},{24,16},{32,24},{40,32},{48,40},{56,48},{64,5... | collective-permute-start | bytes 1769480 | tf_op jit(solution)/shard_map/ppermute | solution.py:44
  7.5 0.4 all_tiles.1
  7.9 0.1 collective-permute-start.2
  7.9 5.3 %collective-permute-start.3 = (f32[256,8,128]{2,1,0:T(8,128)S(1)}, f32[256,8,128]{2,1,0:T(8,128)S(1)}, u32[]{:S(2)}, u32[]{:S(2)}) collective-permute-start(f32[256,8,128]{2,1,0:T(8,128)S(1)} %get-tuple-element.27.refs_1_.mid_ref), channel_id=1, source_target_pairs={{0,120},{8,0},{16,8},{24,16},{32,24},{40,32},{48,40},{56,48},{64,5... | collective-permute-start | bytes 3145736 | tf_op jit(solution)/shard_map/ppermute | solution.py:44
  13.3 8.5 %collective-permute-done.4.refs_0_.lo_ref = f32[144,8,128]{2,1,0:T(8,128)S(1)} collective-permute-done((f32[144,8,128]{2,1,0:T(8,128)}, f32[144,8,128]{2,1,0:T(8,128)S(1)}, u32[]{:S(2)}, u32[]{:S(2)}) %collective-permute-start.4) | collective-permute-done | bytes 589856 | tf_op jit(solution)/shard_map/ppermute | solution.py:43
  21.8 0.1 pack_sides.4
  21.9 0.0 collective-permute-start.6
  22.0 3.0 %collective-permute-start.7 = (f32[128,8,128]{2,1,0:T(8,128)S(1)}, f32[128,8,128]{2,1,0:T(8,128)S(1)}, u32[]{:S(2)}, u32[]{:S(2)}) collective-permute-start(f32[128,8,128]{2,1,0:T(8,128)S(1)} %get-tuple-element.30), channel_id=1, source_target_pairs={{0,7},{1,0},{2,1},{3,2},{4,3},{5,4},{6,5},{7,6},{8,15},{9,8},{10,9... | collective-permute-start | bytes 1572872 | tf_op jit(solution)/shard_map/ppermute | solution.py:44
  25.0 9.5 %collective-permute-done.refs_0_ = f32[64,8,128]{2,1,0:T(8,128)S(1)} collective-permute-done((f32[64,8,128]{2,1,0:T(8,128)S(1)}, f32[64,8,128]{2,1,0:T(8,128)S(1)}, u32[]{:S(2)}, u32[]{:S(2)}) %collective-permute-start) | collective-permute-done | bytes 262176 | tf_op jit(solution)/shard_map/ppermute | solution.py:43
  34.5 5.4 %collective-permute-start.9 = (f32[128,8,128]{2,1,0:T(8,128)S(1)}, f32[128,8,128]{2,1,0:T(8,128)S(1)}, u32[]{:S(2)}, u32[]{:S(2)}) collective-permute-start(f32[128,8,128]{2,1,0:T(8,128)S(1)} %get-tuple-element.33.refs_1_.mid_ref), channel_id=1, source_target_pairs={{0,120},{8,0},{16,8},{24,16},{32,24},{40,32},{48,40},{56,48},{64,5... | collective-permute-start | bytes 1572872 | tf_op jit(solution)/shard_map/ppermute | solution.py:44
  39.9 4.3 %filter_orbitals.4 = (f32[8,8,16,128]{3,2,1,0:T(8,128)S(1)}, f32[24,32,128]{2,1,0:T(8,128)S(1)}) custom-call(f32[144,8,128]{2,1,0:T(8,128)S(1)} %collective-permute-done.4.refs_0_.lo_ref, f32[144,8,128]{2,1,0:T(8,128)S(1)} %get-tuple-element.28.refs_1_.mid_ref, f32[144,8,128]{2,1,0:T(8,128)S(1)} %collective-permute-done.5.refs_2_.hi_ref, ...), custom_call_target="tpu_custom_call" | custom-call | bytes 100 | tf_op jit(solution)/shard_map/filter_orbitals/pallas_call | solution.py:305
  44.3 0.5 gram_rows.4.refs_4_
  44.7 0.0 collective-permute-done.1.refs_1_
  44.8 0.5 collective-permute-start.10
  45.3 2.5 %collective-permute-start.11 = (f32[48,8,128]{2,1,0:T(8,128)S(1)}, f32[48,8,128]{2,1,0:T(8,128)S(1)}, u32[]{:S(2)}, u32[]{:S(2)}) collective-permute-start(f32[48,8,128]{2,1,0:T(8,128)S(1)} %get-tuple-element.37), channel_id=1, source_target_pairs={{0,7},{1,0},{2,1},{3,2},{4,3},{5,4},{6,5},{7,6},{8,15},{9,8},{10,9... | collective-permute-start | bytes 589832 | tf_op jit(solution)/shard_map/ppermute | solution.py:44
  47.9 0.1 pack_sides.6
  48.0 3.2 %collective-permute-done.10.yl_ref = f32[48,8,128]{2,1,0:T(8,128)S(1)} collective-permute-done((f32[48,8,128]{2,1,0:T(8,128)S(1)}, f32[48,8,128]{2,1,0:T(8,128)S(1)}, u32[]{:S(2)}, u32[]{:S(2)}) %collective-permute-start.10) | collective-permute-done | bytes 196640 | tf_op jit(solution)/shard_map/ppermute | solution.py:43
  51.2 4.3 %filter_orbitals.5.refs_1_ = f32[8,8,16,128]{3,2,1,0:T(8,128)S(1)} custom-call(f32[256,8,128]{2,1,0:T(8,128)S(1)} %collective-permute-done.2.refs_0_.lo_ref, f32[256,8,128]{2,1,0:T(8,128)S(1)} %get-tuple-element.27.refs_1_.mid_ref, f32[256,8,128]{2,1,0:T(8,128)S(1)} %collective-permute-done.3.refs_2_.hi_ref, ...), custom_call_target="tpu_custom_call" | custom-call | bytes 100 | tf_op jit(solution)/shard_map/filter_orbitals/pallas_call | solution.py:305
  55.6 0.1 pack_sides.7
  55.6 0.6 collective-permute-start.14
  56.3 2.6 %collective-permute-start.15 = (f32[112,8,128]{2,1,0:T(8,128)S(1)}, f32[112,8,128]{2,1,0:T(8,128)S(1)}, u32[]{:S(2)}, u32[]{:S(2)}) collective-permute-start(f32[112,8,128]{2,1,0:T(8,128)S(1)} %get-tuple-element.47), channel_id=1, source_target_pairs={{0,7},{1,0},{2,1},{3,2},{4,3},{5,4},{6,5},{7,6},{8,15},{9,8},{10,9... | collective-permute-start | bytes 1376264 | tf_op jit(solution)/shard_map/ppermute | solution.py:44
  58.9 0.8 gram_rows.5.refs_5_
  59.8 4.5 %filter_orbitals.6.refs_2_ = f32[8,8,16,128]{3,2,1,0:T(8,128)S(1)} custom-call(f32[256,8,128]{2,1,0:T(8,128)S(1)} %collective-permute-done.2.refs_0_.lo_ref, f32[256,8,128]{2,1,0:T(8,128)S(1)} %get-tuple-element.27.refs_1_.mid_ref, f32[256,8,128]{2,1,0:T(8,128)S(1)} %collective-permute-done.3.refs_2_.hi_ref, ...), custom_call_target="tpu_custom_call" | custom-call | bytes 100 | tf_op jit(solution)/shard_map/filter_orbitals/pallas_call | solution.py:305
  64.3 1.1 %gram_rows.6.refs_6_ = f32[8,128]{1,0:T(8,128)S(1)} custom-call(f32[8,8,16,128]{3,2,1,0:T(8,128)S(1)} %get-tuple-element.32.refs_0_, f32[8,8,16,128]{3,2,1,0:T(8,128)S(1)} %filter_orbitals.5.refs_1_, f32[8,8,16,128]{3,2,1,0:T(8,128)S(1)} %filter_orbitals.6.refs_2_), custom_call_target="tpu_custom_call" | custom-call | bytes 100 | tf_op jit(solution)/shard_map/gram_rows/pallas_call | solution.py:373
  65.4 4.3 %filter_orbitals.7.refs_3_ = f32[8,8,16,128]{3,2,1,0:T(8,128)S(1)} custom-call(f32[128,8,128]{2,1,0:T(8,128)S(1)} %collective-permute-done.8.refs_0_.lo_ref, f32[128,8,128]{2,1,0:T(8,128)S(1)} %get-tuple-element.33.refs_1_.mid_ref, f32[128,8,128]{2,1,0:T(8,128)S(1)} %collective-permute-done.9.refs_2_.hi_ref, ...), custom_call_target="tpu_custom_call" | custom-call | bytes 100 | tf_op jit(solution)/shard_map/filter_orbitals/pallas_call | solution.py:305
  69.8 1.4 %gram_rows.7 = f32[8,128]{1,0:T(8,128)S(1)} custom-call(f32[8,8,16,128]{3,2,1,0:T(8,128)S(1)} %get-tuple-element.32.refs_0_, f32[8,8,16,128]{3,2,1,0:T(8,128)S(1)} %filter_orbitals.5.refs_1_, f32[8,8,16,128]{3,2,1,0:T(8,128)S(1)} %filter_orbitals.6.refs_2_, f32[8,8,16,128]{3,2,1,0:T(8,128)S(1)} %filter_orbitals.7.refs_3_, f32[8,128]{1,0:T(8,128)S(1)} %gram_rows.4.refs_4_, ...), custom_call_target="tpu_custom_call" | custom-call | bytes 100 | tf_op jit(solution)/shard_map/gram_rows/pallas_call | solution.py:373
  71.2 0.1 collective-permute-start.16
  71.3 1.2 %collective-permute-done.16 = f32[8,128]{1,0:T(8,128)S(1)} collective-permute-done((f32[8,128]{1,0:T(8,128)S(1)}, f32[8,128]{1,0:T(8,128)S(1)}, u32[]{:S(2)}, u32[]{:S(2)}) %collective-permute-start.16) | collective-permute-done | bytes 4128 | tf_op jit(solution)/shard_map/ppermute | solution.py:500
  72.5 20.2 %all_to_all.5.recv_ref = f32[64,8,128]{2,1,0:T(8,128)S(1)} all-to-all(f32[64,8,128]{2,1,0:T(8,128)S(1)} %broadcast_in_dim.2), channel_id=1, replica_groups=mesh['gx'=16,'gz'=4,'core'=2] {'gx','gz'}, dimensions={0} | all-to-all | bytes 524288 | tf_op jit(solution)/shard_map/all_to_all | solution.py:502
  92.7 3.9 %orthonormalize.1 = f32[32,8,16,128]{3,2,1,0:T(8,128)} custom-call(f32[64,8,128]{2,1,0:T(8,128)S(1)} %all_to_all.5.recv_ref, f32[8,8,16,128]{3,2,1,0:T(8,128)S(1)} %get-tuple-element.32.refs_0_, f32[8,8,16,128]{3,2,1,0:T(8,128)S(1)} %filter_orbitals.5.refs_1_, f32[8,8,16,128]{3,2,1,0:T(8,128)S(1)} %filter_orbitals.6.refs_2_, ...), custom_call_target="tpu_custom_call" | custom-call | tf_op jit(solution)/shard_map/orthonormalize/pallas_call | solution.py:439
  (26 shorter events, 0.2 us)
Async XLA Ops:
  0.0 7.5 %copy-start = (f32[32,8,16,128]{3,2,1,0:T(8,128)S(1)}, f32[32,8,16,128]{3,2,1,0:T(8,128)}, u32[]{:S(2)}) copy-start(f32[32,8,16,128]{3,2,1,0:T(8,128)} %orb_ref.3) | copy-start | bytes 6291460
  0.0 7.5 %copy-start.1 = (f32[8,16,128]{2,1,0:T(8,128)S(1)}, f32[8,16,128]{2,1,0:T(8,128)}, u32[]{:S(2)}) copy-start(f32[8,16,128]{2,1,0:T(8,128)} %pot_ref.3) | copy-start | bytes 196612
  2.0 19.8 %collective-permute-start.4 = (f32[144,8,128]{2,1,0:T(8,128)}, f32[144,8,128]{2,1,0:T(8,128)S(1)}, u32[]{:S(2)}, u32[]{:S(2)}) collective-permute-start(f32[144,8,128]{2,1,0:T(8,128)} %first_tiles.1), channel_id=1, source_target_pairs={{0,8},{8,16},{16,24},{24,32},{32,40},{40,48},{48,56},{56,64},{64,7... | collective-permute-start | bytes 1769480 | tf_op jit(solution)/shard_map/ppermute | solution.py:43
  3.7 18.1 %collective-permute-start.5 = (f32[144,8,128]{2,1,0:T(8,128)}, f32[144,8,128]{2,1,0:T(8,128)S(1)}, u32[]{:S(2)}, u32[]{:S(2)}) collective-permute-start(f32[144,8,128]{2,1,0:T(8,128)} %first_tiles.1), channel_id=1, source_target_pairs={{0,120},{8,0},{16,8},{24,16},{32,24},{40,32},{48,40},{56,48},{64,5... | collective-permute-start | bytes 1769480 | tf_op jit(solution)/shard_map/ppermute | solution.py:44
  7.9 36.9 %collective-permute-start.2 = (f32[256,8,128]{2,1,0:T(8,128)S(1)}, f32[256,8,128]{2,1,0:T(8,128)S(1)}, u32[]{:S(2)}, u32[]{:S(2)}) collective-permute-start(f32[256,8,128]{2,1,0:T(8,128)S(1)} %get-tuple-element.27.refs_1_.mid_ref), channel_id=1, source_target_pairs={{0,8},{8,16},{16,24},{24,32},{32,40},{40,48},{48,56},{56,64},{64,7... | collective-permute-start | bytes 3145736 | tf_op jit(solution)/shard_map/ppermute | solution.py:43
  7.9 36.8 %collective-permute-start.3 = (f32[256,8,128]{2,1,0:T(8,128)S(1)}, f32[256,8,128]{2,1,0:T(8,128)S(1)}, u32[]{:S(2)}, u32[]{:S(2)}) collective-permute-start(f32[256,8,128]{2,1,0:T(8,128)S(1)} %get-tuple-element.27.refs_1_.mid_ref), channel_id=1, source_target_pairs={{0,120},{8,0},{16,8},{24,16},{32,24},{40,32},{48,40},{56,48},{64,5... | collective-permute-start | bytes 3145736 | tf_op jit(solution)/shard_map/ppermute | solution.py:44
  21.9 12.6 %collective-permute-start.6 = (f32[128,8,128]{2,1,0:T(8,128)S(1)}, f32[128,8,128]{2,1,0:T(8,128)S(1)}, u32[]{:S(2)}, u32[]{:S(2)}) collective-permute-start(f32[128,8,128]{2,1,0:T(8,128)S(1)} %get-tuple-element.29), channel_id=1, source_target_pairs={{0,1},{1,2},{2,3},{3,4},{4,5},{5,6},{6,7},{7,0},{8,9},{9,10},{10,1... | collective-permute-start | bytes 1572872 | tf_op jit(solution)/shard_map/ppermute | solution.py:43
  22.0 18.0 %collective-permute-start.7 = (f32[128,8,128]{2,1,0:T(8,128)S(1)}, f32[128,8,128]{2,1,0:T(8,128)S(1)}, u32[]{:S(2)}, u32[]{:S(2)}) collective-permute-start(f32[128,8,128]{2,1,0:T(8,128)S(1)} %get-tuple-element.30), channel_id=1, source_target_pairs={{0,7},{1,0},{2,1},{3,2},{4,3},{5,4},{6,5},{7,6},{8,15},{9,8},{10,9... | collective-permute-start | bytes 1572872 | tf_op jit(solution)/shard_map/ppermute | solution.py:44
  25.0 9.6 %collective-permute-start = (f32[64,8,128]{2,1,0:T(8,128)S(1)}, f32[64,8,128]{2,1,0:T(8,128)S(1)}, u32[]{:S(2)}, u32[]{:S(2)}) collective-permute-start(f32[64,8,128]{2,1,0:T(8,128)S(1)} %bitcast.5), channel_id=1, source_target_pairs={{0,1},{1,2},{2,3},{3,4},{4,5},{5,6},{6,7},{7,0},{8,9},{9,10},{10,1... | collective-permute-start | bytes 786440 | tf_op jit(solution)/shard_map/ppermute | solution.py:43
  34.5 21.0 %collective-permute-start.8 = (f32[128,8,128]{2,1,0:T(8,128)S(1)}, f32[128,8,128]{2,1,0:T(8,128)S(1)}, u32[]{:S(2)}, u32[]{:S(2)}) collective-permute-start(f32[128,8,128]{2,1,0:T(8,128)S(1)} %get-tuple-element.33.refs_1_.mid_ref), channel_id=1, source_target_pairs={{0,8},{8,16},{16,24},{24,32},{32,40},{40,48},{48,56},{56,64},{64,7... | collective-permute-start | bytes 1572872 | tf_op jit(solution)/shard_map/ppermute | solution.py:43
  34.5 21.0 %collective-permute-start.9 = (f32[128,8,128]{2,1,0:T(8,128)S(1)}, f32[128,8,128]{2,1,0:T(8,128)S(1)}, u32[]{:S(2)}, u32[]{:S(2)}) collective-permute-start(f32[128,8,128]{2,1,0:T(8,128)S(1)} %get-tuple-element.33.refs_1_.mid_ref), channel_id=1, source_target_pairs={{0,120},{8,0},{16,8},{24,16},{32,24},{40,32},{48,40},{56,48},{64,5... | collective-permute-start | bytes 1572872 | tf_op jit(solution)/shard_map/ppermute | solution.py:44
  39.9 4.8 %collective-permute-start.1 = (f32[64,8,128]{2,1,0:T(8,128)S(1)}, f32[64,8,128]{2,1,0:T(8,128)S(1)}, u32[]{:S(2)}, u32[]{:S(2)}) collective-permute-start(f32[64,8,128]{2,1,0:T(8,128)S(1)} %bitcast.4), channel_id=1, source_target_pairs={{0,7},{1,0},{2,1},{3,2},{4,3},{5,4},{6,5},{7,6},{8,15},{9,8},{10,9... | collective-permute-start | bytes 786440 | tf_op jit(solution)/shard_map/ppermute | solution.py:44
  44.8 6.4 %collective-permute-start.10 = (f32[48,8,128]{2,1,0:T(8,128)S(1)}, f32[48,8,128]{2,1,0:T(8,128)S(1)}, u32[]{:S(2)}, u32[]{:S(2)}) collective-permute-start(f32[48,8,128]{2,1,0:T(8,128)S(1)} %get-tuple-element.36), channel_id=1, source_target_pairs={{0,1},{1,2},{2,3},{3,4},{4,5},{5,6},{6,7},{7,0},{8,9},{9,10},{10,1... | collective-permute-start | bytes 589832 | tf_op jit(solution)/shard_map/ppermute | solution.py:43
  45.3 5.9 %collective-permute-start.11 = (f32[48,8,128]{2,1,0:T(8,128)S(1)}, f32[48,8,128]{2,1,0:T(8,128)S(1)}, u32[]{:S(2)}, u32[]{:S(2)}) collective-permute-start(f32[48,8,128]{2,1,0:T(8,128)S(1)} %get-tuple-element.37), channel_id=1, source_target_pairs={{0,7},{1,0},{2,1},{3,2},{4,3},{5,4},{6,5},{7,6},{8,15},{9,8},{10,9... | collective-permute-start | bytes 589832 | tf_op jit(solution)/shard_map/ppermute | solution.py:44
  47.9 11.8 %collective-permute-start.12 = (f32[112,8,128]{2,1,0:T(8,128)S(1)}, f32[112,8,128]{2,1,0:T(8,128)S(1)}, u32[]{:S(2)}, u32[]{:S(2)}) collective-permute-start(f32[112,8,128]{2,1,0:T(8,128)S(1)} %get-tuple-element.42), channel_id=1, source_target_pairs={{0,1},{1,2},{2,3},{3,4},{4,5},{5,6},{6,7},{7,0},{8,9},{9,10},{10,1... | collective-permute-start | bytes 1376264 | tf_op jit(solution)/shard_map/ppermute | solution.py:43
  51.2 8.5 %collective-permute-start.13 = (f32[112,8,128]{2,1,0:T(8,128)S(1)}, f32[112,8,128]{2,1,0:T(8,128)S(1)}, u32[]{:S(2)}, u32[]{:S(2)}) collective-permute-start(f32[112,8,128]{2,1,0:T(8,128)S(1)} %get-tuple-element.43), channel_id=1, source_target_pairs={{0,7},{1,0},{2,1},{3,2},{4,3},{5,4},{6,5},{7,6},{8,15},{9,8},{10,9... | collective-permute-start | bytes 1376264 | tf_op jit(solution)/shard_map/ppermute | solution.py:44
  55.6 9.8 %collective-permute-start.14 = (f32[112,8,128]{2,1,0:T(8,128)S(1)}, f32[112,8,128]{2,1,0:T(8,128)S(1)}, u32[]{:S(2)}, u32[]{:S(2)}) collective-permute-start(f32[112,8,128]{2,1,0:T(8,128)S(1)} %get-tuple-element.46), channel_id=1, source_target_pairs={{0,1},{1,2},{2,3},{3,4},{4,5},{5,6},{6,7},{7,0},{8,9},{9,10},{10,1... | collective-permute-start | bytes 1376264 | tf_op jit(solution)/shard_map/ppermute | solution.py:43
  56.3 9.1 %collective-permute-start.15 = (f32[112,8,128]{2,1,0:T(8,128)S(1)}, f32[112,8,128]{2,1,0:T(8,128)S(1)}, u32[]{:S(2)}, u32[]{:S(2)}) collective-permute-start(f32[112,8,128]{2,1,0:T(8,128)S(1)} %get-tuple-element.47), channel_id=1, source_target_pairs={{0,7},{1,0},{2,1},{3,2},{4,3},{5,4},{6,5},{7,6},{8,15},{9,8},{10,9... | collective-permute-start | bytes 1376264 | tf_op jit(solution)/shard_map/ppermute | solution.py:44
  71.2 1.2 %collective-permute-start.16 = (f32[8,128]{1,0:T(8,128)S(1)}, f32[8,128]{1,0:T(8,128)S(1)}, u32[]{:S(2)}, u32[]{:S(2)}) collective-permute-start(f32[8,128]{1,0:T(8,128)S(1)} %gram_rows.7), channel_id=1, source_target_pairs={{0,1},{1,0},{2,3},{3,2},{4,5},{5,4},{6,7},{7,6},{8,9},{9,8},{10,11... | collective-permute-start | bytes 12296 | tf_op jit(solution)/shard_map/ppermute | solution.py:500

commit v2 on v1

--- a/solution.py
+++ b/solution.py
@@ -23,7 +23,7 @@
 UNITS = ((0, 0, 1), (1, 0, 1), (1, 1, 1), (2, 0, 1))
 AFTER = {1: 0, 3: 1}
 RIDES = {}
-ALONE = (1,)
+ALONE = (0, 1)
 FILTER_COST = 100
 GY = ("gz", "core")
 CORES = 2
@@ -262,7 +262,7 @@
         for x in range(cx):
             sides[HALO + x] = (refs[0], refs[1], own_at + x * HALO, HALO)
     if first:
-        out_ref, diag_ref = refs[:2]
+        out_ref, diag_ref = refs[-5:-3]
         per = cy // 8
         cz = out_ref.shape[-1]
         for x in range(cx):
@@ -464,19 +464,24 @@
     filtered, grams, all_sides, alone = [], [], [], {}
     for index, (chunk, start, groups) in enumerate(UNITS):
         unit = (start, groups, index == 0, index in RIDES or index in ALONE)
-        if index in AFTER:
+        if index in AFTER or index in ALONE:
             lo, mid, hi = blocks[chunk]
-            before = AFTER[index]
-            tied = (lo, hi, filtered[before]) + ((grams[before],) if before == 0 else ())
+            tied = (lo, hi)
             if index in ALONE:
                 part = mid[start * cx * cy :][: cx * cy].reshape((cx, cy) + mid.shape[1:])
                 rows = [p.reshape((cx * HALO,) + p.shape[2:]) for p in (part[:, :HALO], part[:, cy - HALO :])]
-                tied = both_ways(*rows, GY) + tied
+                tied += both_ways(*rows, GY)
+            size = len(tied)
+            before = AFTER.get(index)
+            if before is not None:
+                tied += (filtered[before],) + ((grams[before],) if before == 0 else ())
             tied = lax.optimization_barrier(tied)
+            lo, hi = tied[:2]
             if index in ALONE:
-                alone[index], tied = tied[:2], tied[2:]
-            lo, hi, filtered[before], *rest = tied
-            grams[before : before + len(rest)] = rest
+                alone[index] = tied[2:4]
+            if before is not None:
+                filtered[before], *rest = tied[size:]
+                grams[before : before + len(rest)] = rest
             blocks[chunk] = lo, mid, hi
         rider, rider_mid = None, None
         for later, carrier in RIDES.items():

time: 96.9 us -> 96.9 us (level)
  waiting for transfers between devices: 22.5 us -> 21.5 us
    ppermute x8 -> x9, waiting for transfers between devices: 21.3 us -> 16.5 us  [both_ways(): lax.ppermute(high_part, axis, shift_perm(axis, 1))]
    ppermute x8 -> x9, waiting for transfers between devices: 0.04 us -> 3.85 us  [both_ways(): lax.ppermute(low_part, axis, shift_perm(axis, -1))]
    ppermute x8 -> x9, starting transfers between devices: 2.94 us -> 4.02 us  [both_ways(): lax.ppermute(high_part, axis, shift_perm(axis, 1))]
    ppermute x8 -> x9, starting transfers between devices: 22.7 us -> 22 us  [both_ways(): lax.ppermute(low_part, axis, shift_perm(axis, -1))]
  transfers between devices with their start and end apart: 17 -> 19, of which waited for: 4 -> 8; matrix products, arithmetic and copies ran while one was open for 0% -> 0% of each run, Pallas kernels for 17% -> 17%
where the time goes in v2:
time: 96.9 us; the launch traced here: 96.8 us
  Pallas kernels  27.8 us (29%)
  starting transfers between devices  26.1 us (27%)
  waiting for transfers between devices  21.5 us (22%)
  blocking collectives  20.7 us (21%)
    ppermute x9, starting transfers between devices, both_ways(): lax.ppermute(low_part, axis, shift_perm(axis, -1))  22 us
    all_to_all x1, blocking collectives, body(): received = lax.all_to_all(chip, ('gx', 'gz'), 0, 0, tiled=True)  20.7 us
    pallas_call x4, Pallas kernels, run_filter(): pl.pallas_call(functools.partial(filter_kernel, unit, chunk_groups, own_a...  17.5 us
    ppermute x9, waiting for transfers between devices, both_ways(): lax.ppermute(high_part, axis, shift_perm(axis, 1))  16.5 us
    ppermute x9, starting transfers between devices, both_ways(): lax.ppermute(high_part, axis, shift_perm(axis, 1))  4.02 us
    pallas_call x1, Pallas kernels, run_solve(): pl.pallas_call(functools.partial(solve_kernel, counts), out_shape=jax.Sha...  3.88 us
    ppermute x9, waiting for transfers between devices, both_ways(): lax.ppermute(low_part, axis, shift_perm(axis, -1))  3.85 us
    pallas_call x4, Pallas kernels, run_gram(): pl.pallas_call(functools.partial(gram_kernel, offset, scale, counts), out...  3.79 us
  transfers between devices with their start and end apart: 19, of which 8 were waited for; matrix products, arithmetic and copies ran while one was open for 0% of the time, Pallas kernels for 17%

profile of v2, /device:TPU:0, one launch (start us, length us, event | category | flops | bytes accessed | tf_op | source)
XLA Modules:
  0.0 96.8 jit_solution(8194173731674321273)
XLA Ops:
  0.0 2.0 %first_tiles.1 = f32[144,8,128]{2,1,0:T(8,128)} custom-call(f32[8,16,128]{2,1,0:T(8,128)} %pot_ref.3, f32[32,8,16,128]{3,2,1,0:T(8,128)} %orb_ref.3), custom_call_target="tpu_custom_call" | custom-call | tf_op jit(solution)/shard_map/first_tiles/pallas_call | solution.py:111
  2.0 1.6 %collective-permute-start.4 = (f32[144,8,128]{2,1,0:T(8,128)}, f32[144,8,128]{2,1,0:T(8,128)S(1)}, u32[]{:S(2)}, u32[]{:S(2)}) collective-permute-start(f32[144,8,128]{2,1,0:T(8,128)} %first_tiles.1), channel_id=1, source_target_pairs={{0,8},{8,16},{16,24},{24,32},{32,40},{40,48},{48,56},{56,64},{64,7... | collective-permute-start | bytes 1769480 | tf_op jit(solution)/shard_map/ppermute | solution.py:43
  3.7 3.8 %collective-permute-start.5 = (f32[144,8,128]{2,1,0:T(8,128)}, f32[144,8,128]{2,1,0:T(8,128)S(1)}, u32[]{:S(2)}, u32[]{:S(2)}) collective-permute-start(f32[144,8,128]{2,1,0:T(8,128)} %first_tiles.1), channel_id=1, source_target_pairs={{0,120},{8,0},{16,8},{24,16},{32,24},{40,32},{48,40},{56,48},{64,5... | collective-permute-start | bytes 1769480 | tf_op jit(solution)/shard_map/ppermute | solution.py:44
  7.5 0.4 all_tiles.1
  8.0 0.1 collective-permute-start
  8.1 5.3 %collective-permute-start.1 = (f32[256,8,128]{2,1,0:T(8,128)S(1)}, f32[256,8,128]{2,1,0:T(8,128)S(1)}, u32[]{:S(2)}, u32[]{:S(2)}) collective-permute-start(f32[256,8,128]{2,1,0:T(8,128)S(1)} %get-tuple-element.31.refs_1_.mid_ref), channel_id=1, source_target_pairs={{0,120},{8,0},{16,8},{24,16},{32,24},{40,32},{48,40},{56,48},{64,5... | collective-permute-start | bytes 3145736 | tf_op jit(solution)/shard_map/ppermute | solution.py:44
  13.4 1.8 %collective-permute-done.6.refs_0_ = f32[64,8,128]{2,1,0:T(8,128)S(1)} collective-permute-done((f32[64,8,128]{2,1,0:T(8,128)S(1)}, f32[64,8,128]{2,1,0:T(8,128)S(1)}, u32[]{:S(2)}, u32[]{:S(2)}) %collective-permute-start.6) | collective-permute-done | bytes 262176 | tf_op jit(solution)/shard_map/ppermute | solution.py:43
  15.2 0.8 collective-permute-start.7
  16.1 3.8 %collective-permute-done.7.refs_1_ = f32[64,8,128]{2,1,0:T(8,128)S(1)} collective-permute-done((f32[64,8,128]{2,1,0:T(8,128)S(1)}, f32[64,8,128]{2,1,0:T(8,128)S(1)}, u32[]{:S(2)}, u32[]{:S(2)}) %collective-permute-start.7) | collective-permute-done | bytes 262176 | tf_op jit(solution)/shard_map/ppermute | solution.py:44
  19.9 1.0 %collective-permute-start.2 = (f32[64,8,128]{2,1,0:T(8,128)S(1)}, f32[64,8,128]{2,1,0:T(8,128)S(1)}, u32[]{:S(2)}, u32[]{:S(2)}) collective-permute-start(f32[64,8,128]{2,1,0:T(8,128)S(1)} %bitcast.9), channel_id=1, source_target_pairs={{0,1},{1,2},{2,3},{3,4},{4,5},{5,6},{6,7},{7,0},{8,9},{9,10},{10,1... | collective-permute-start | bytes 786440 | tf_op jit(solution)/shard_map/ppermute | solution.py:43
  20.9 0.9 collective-permute-done.4.refs_0_.lo_ref
  21.9 2.9 %collective-permute-start.9 = (f32[64,8,128]{2,1,0:T(8,128)S(1)}, f32[64,8,128]{2,1,0:T(8,128)S(1)}, u32[]{:S(2)}, u32[]{:S(2)}) collective-permute-start(f32[64,8,128]{2,1,0:T(8,128)S(1)} %get-tuple-element.36), channel_id=1, source_target_pairs={{0,7},{1,0},{2,1},{3,2},{4,3},{5,4},{6,5},{7,6},{8,15},{9,8},{10,9... | collective-permute-start | bytes 786440 | tf_op jit(solution)/shard_map/ppermute | solution.py:44
  24.8 2.6 %collective-permute-done.2.refs_0_ = f32[64,8,128]{2,1,0:T(8,128)S(1)} collective-permute-done((f32[64,8,128]{2,1,0:T(8,128)S(1)}, f32[64,8,128]{2,1,0:T(8,128)S(1)}, u32[]{:S(2)}, u32[]{:S(2)}) %collective-permute-start.2) | collective-permute-done | bytes 262176 | tf_op jit(solution)/shard_map/ppermute | solution.py:43
  27.4 2.8 %collective-permute-done.8.yl_ref = f32[64,8,128]{2,1,0:T(8,128)S(1)} collective-permute-done((f32[64,8,128]{2,1,0:T(8,128)S(1)}, f32[64,8,128]{2,1,0:T(8,128)S(1)}, u32[]{:S(2)}, u32[]{:S(2)}) %collective-permute-start.8) | collective-permute-done | bytes 262176 | tf_op jit(solution)/shard_map/ppermute | solution.py:43
  30.2 4.1 %collective-permute-start.11 = (f32[128,8,128]{2,1,0:T(8,128)S(1)}, f32[128,8,128]{2,1,0:T(8,128)S(1)}, u32[]{:S(2)}, u32[]{:S(2)}) collective-permute-start(f32[128,8,128]{2,1,0:T(8,128)S(1)} %get-tuple-element.41.refs_1_.mid_ref), channel_id=1, source_target_pairs={{0,120},{8,0},{16,8},{24,16},{32,24},{40,32},{48,40},{56,48},{64,5... | collective-permute-start | bytes 1572872 | tf_op jit(solution)/shard_map/ppermute | solution.py:44
  34.3 4.3 %filter_orbitals.4 = (f32[8,8,16,128]{3,2,1,0:T(8,128)S(1)}, f32[24,32,128]{2,1,0:T(8,128)S(1)}) custom-call(f32[144,8,128]{2,1,0:T(8,128)S(1)} %collective-permute-done.4.refs_0_.lo_ref, f32[144,8,128]{2,1,0:T(8,128)S(1)} %get-tuple-element.32.refs_1_.mid_ref, f32[144,8,128]{2,1,0:T(8,128)S(1)} %collective-permute-done.5.refs_2_.hi_ref, ...), custom_call_target="tpu_custom_call" | custom-call | bytes 100 | tf_op jit(solution)/shard_map/filter_orbitals/pallas_call | solution.py:305
  38.6 0.5 gram_rows.4.refs_4_
  39.1 5.2 %collective-permute-done.refs_0_.lo_ref = f32[256,8,128]{2,1,0:T(8,128)S(1)} collective-permute-done((f32[256,8,128]{2,1,0:T(8,128)S(1)}, f32[256,8,128]{2,1,0:T(8,128)S(1)}, u32[]{:S(2)}, u32[]{:S(2)}) %collective-permute-start) | collective-permute-done | bytes 1048608 | tf_op jit(solution)/shard_map/ppermute | solution.py:43
  44.3 2.9 %collective-permute-start.13 = (f32[48,8,128]{2,1,0:T(8,128)S(1)}, f32[48,8,128]{2,1,0:T(8,128)S(1)}, u32[]{:S(2)}, u32[]{:S(2)}) collective-permute-start(f32[48,8,128]{2,1,0:T(8,128)S(1)} %get-tuple-element.45), channel_id=1, source_target_pairs={{0,7},{1,0},{2,1},{3,2},{4,3},{5,4},{6,5},{7,6},{8,15},{9,8},{10,9... | collective-permute-start | bytes 589832 | tf_op jit(solution)/shard_map/ppermute | solution.py:44
  47.4 3.3 %collective-permute-done.12.yl_ref = f32[48,8,128]{2,1,0:T(8,128)S(1)} collective-permute-done((f32[48,8,128]{2,1,0:T(8,128)S(1)}, f32[48,8,128]{2,1,0:T(8,128)S(1)}, u32[]{:S(2)}, u32[]{:S(2)}) %collective-permute-start.12) | collective-permute-done | bytes 196640 | tf_op jit(solution)/shard_map/ppermute | solution.py:43
  50.6 4.3 %filter_orbitals.5.refs_1_ = f32[8,8,16,128]{3,2,1,0:T(8,128)S(1)} custom-call(f32[256,8,128]{2,1,0:T(8,128)S(1)} %collective-permute-done.refs_0_.lo_ref, f32[256,8,128]{2,1,0:T(8,128)S(1)} %get-tuple-element.31.refs_1_.mid_ref, f32[256,8,128]{2,1,0:T(8,128)S(1)} %collective-permute-done.1.refs_2_.hi_ref, f32[48,8,128]{2,1,0:T(8,128)S(1)} %collective-permute-done.12.yl_ref, ...), custom_call_target="tpu_custom_call" | custom-call | bytes 100 | tf_op jit(solution)/shard_map/filter_orbitals/pallas_call | solution.py:305
  55.1 1.2 %collective-permute-start.16 = (f32[112,8,128]{2,1,0:T(8,128)S(1)}, f32[112,8,128]{2,1,0:T(8,128)S(1)}, u32[]{:S(2)}, u32[]{:S(2)}) collective-permute-start(f32[112,8,128]{2,1,0:T(8,128)S(1)} %get-tuple-element.54), channel_id=1, source_target_pairs={{0,1},{1,2},{2,3},{3,4},{4,5},{5,6},{6,7},{7,0},{8,9},{9,10},{10,1... | collective-permute-start | bytes 1376264 | tf_op jit(solution)/shard_map/ppermute | solution.py:43
  56.3 2.1 %collective-permute-start.17 = (f32[112,8,128]{2,1,0:T(8,128)S(1)}, f32[112,8,128]{2,1,0:T(8,128)S(1)}, u32[]{:S(2)}, u32[]{:S(2)}) collective-permute-start(f32[112,8,128]{2,1,0:T(8,128)S(1)} %get-tuple-element.55), channel_id=1, source_target_pairs={{0,7},{1,0},{2,1},{3,2},{4,3},{5,4},{6,5},{7,6},{8,15},{9,8},{10,9... | collective-permute-start | bytes 1376264 | tf_op jit(solution)/shard_map/ppermute | solution.py:44
  58.4 0.8 gram_rows.5.refs_5_
  59.2 4.6 %filter_orbitals.6.refs_2_ = f32[8,8,16,128]{3,2,1,0:T(8,128)S(1)} custom-call(f32[256,8,128]{2,1,0:T(8,128)S(1)} %collective-permute-done.refs_0_.lo_ref, f32[256,8,128]{2,1,0:T(8,128)S(1)} %get-tuple-element.31.refs_1_.mid_ref, f32[256,8,128]{2,1,0:T(8,128)S(1)} %collective-permute-done.1.refs_2_.hi_ref, ...), custom_call_target="tpu_custom_call" | custom-call | bytes 100 | tf_op jit(solution)/shard_map/filter_orbitals/pallas_call | solution.py:305
  63.8 1.1 %gram_rows.6.refs_6_ = f32[8,128]{1,0:T(8,128)S(1)} custom-call(f32[8,8,16,128]{3,2,1,0:T(8,128)S(1)} %get-tuple-element.40.refs_0_, f32[8,8,16,128]{3,2,1,0:T(8,128)S(1)} %filter_orbitals.5.refs_1_, f32[8,8,16,128]{3,2,1,0:T(8,128)S(1)} %filter_orbitals.6.refs_2_), custom_call_target="tpu_custom_call" | custom-call | bytes 100 | tf_op jit(solution)/shard_map/gram_rows/pallas_call | solution.py:373
  64.9 4.3 %filter_orbitals.7.refs_3_ = f32[8,8,16,128]{3,2,1,0:T(8,128)S(1)} custom-call(f32[128,8,128]{2,1,0:T(8,128)S(1)} %collective-permute-done.10.refs_0_.lo_ref, f32[128,8,128]{2,1,0:T(8,128)S(1)} %get-tuple-element.41.refs_1_.mid_ref, f32[128,8,128]{2,1,0:T(8,128)S(1)} %collective-permute-done.11.refs_2_.hi_ref, ...), custom_call_target="tpu_custom_call" | custom-call | bytes 100 | tf_op jit(solution)/shard_map/filter_orbitals/pallas_call | solution.py:305
  69.2 1.4 %gram_rows.7 = f32[8,128]{1,0:T(8,128)S(1)} custom-call(f32[8,8,16,128]{3,2,1,0:T(8,128)S(1)} %get-tuple-element.40.refs_0_, f32[8,8,16,128]{3,2,1,0:T(8,128)S(1)} %filter_orbitals.5.refs_1_, f32[8,8,16,128]{3,2,1,0:T(8,128)S(1)} %filter_orbitals.6.refs_2_, f32[8,8,16,128]{3,2,1,0:T(8,128)S(1)} %filter_orbitals.7.refs_3_, f32[8,128]{1,0:T(8,128)S(1)} %gram_rows.4.refs_4_, ...), custom_call_target="tpu_custom_call" | custom-call | bytes 100 | tf_op jit(solution)/shard_map/gram_rows/pallas_call | solution.py:373
  70.7 0.1 collective-permute-start.18
  70.8 1.2 %collective-permute-done.18 = f32[8,128]{1,0:T(8,128)S(1)} collective-permute-done((f32[8,128]{1,0:T(8,128)S(1)}, f32[8,128]{1,0:T(8,128)S(1)}, u32[]{:S(2)}, u32[]{:S(2)}) %collective-permute-start.18) | collective-permute-done | bytes 4128 | tf_op jit(solution)/shard_map/ppermute | solution.py:505
  71.9 20.7 %all_to_all.5.recv_ref = f32[64,8,128]{2,1,0:T(8,128)S(1)} all-to-all(f32[64,8,128]{2,1,0:T(8,128)S(1)} %broadcast_in_dim.2), channel_id=1, replica_groups=mesh['gx'=16,'gz'=4,'core'=2] {'gx','gz'}, dimensions={0} | all-to-all | bytes 524288 | tf_op jit(solution)/shard_map/all_to_all | solution.py:507
  92.7 3.9 %orthonormalize.1 = f32[32,8,16,128]{3,2,1,0:T(8,128)} custom-call(f32[64,8,128]{2,1,0:T(8,128)S(1)} %all_to_all.5.recv_ref, f32[8,8,16,128]{3,2,1,0:T(8,128)S(1)} %get-tuple-element.40.refs_0_, f32[8,8,16,128]{3,2,1,0:T(8,128)S(1)} %filter_orbitals.5.refs_1_, f32[8,8,16,128]{3,2,1,0:T(8,128)S(1)} %filter_orbitals.6.refs_2_, ...), custom_call_target="tpu_custom_call" | custom-call | tf_op jit(solution)/shard_map/orthonormalize/pallas_call | solution.py:439
  (32 shorter events, 0.5 us)
Async XLA Ops:
  0.0 7.5 %copy-start = (f32[32,8,16,128]{3,2,1,0:T(8,128)S(1)}, f32[32,8,16,128]{3,2,1,0:T(8,128)}, u32[]{:S(2)}) copy-start(f32[32,8,16,128]{3,2,1,0:T(8,128)} %orb_ref.3) | copy-start | bytes 6291460
  0.0 7.5 %copy-start.1 = (f32[8,16,128]{2,1,0:T(8,128)S(1)}, f32[8,16,128]{2,1,0:T(8,128)}, u32[]{:S(2)}) copy-start(f32[8,16,128]{2,1,0:T(8,128)} %pot_ref.3) | copy-start | bytes 196612
  2.0 19.8 %collective-permute-start.4 = (f32[144,8,128]{2,1,0:T(8,128)}, f32[144,8,128]{2,1,0:T(8,128)S(1)}, u32[]{:S(2)}, u32[]{:S(2)}) collective-permute-start(f32[144,8,128]{2,1,0:T(8,128)} %first_tiles.1), channel_id=1, source_target_pairs={{0,8},{8,16},{16,24},{24,32},{32,40},{40,48},{48,56},{56,64},{64,7... | collective-permute-start | bytes 1769480 | tf_op jit(solution)/shard_map/ppermute | solution.py:43
  3.7 18.1 %collective-permute-start.5 = (f32[144,8,128]{2,1,0:T(8,128)}, f32[144,8,128]{2,1,0:T(8,128)S(1)}, u32[]{:S(2)}, u32[]{:S(2)}) collective-permute-start(f32[144,8,128]{2,1,0:T(8,128)} %first_tiles.1), channel_id=1, source_target_pairs={{0,120},{8,0},{16,8},{24,16},{32,24},{40,32},{48,40},{56,48},{64,5... | collective-permute-start | bytes 1769480 | tf_op jit(solution)/shard_map/ppermute | solution.py:44
  8.0 7.3 %collective-permute-start.6 = (f32[64,8,128]{2,1,0:T(8,128)S(1)}, f32[64,8,128]{2,1,0:T(8,128)S(1)}, u32[]{:S(2)}, u32[]{:S(2)}) collective-permute-start(f32[64,8,128]{2,1,0:T(8,128)S(1)} %bitcast.11), channel_id=1, source_target_pairs={{0,1},{1,2},{2,3},{3,4},{4,5},{5,6},{6,7},{7,0},{8,9},{9,10},{10,1... | collective-permute-start | bytes 786440 | tf_op jit(solution)/shard_map/ppermute | solution.py:43
  8.0 36.3 %collective-permute-start = (f32[256,8,128]{2,1,0:T(8,128)S(1)}, f32[256,8,128]{2,1,0:T(8,128)S(1)}, u32[]{:S(2)}, u32[]{:S(2)}) collective-permute-start(f32[256,8,128]{2,1,0:T(8,128)S(1)} %get-tuple-element.31.refs_1_.mid_ref), channel_id=1, source_target_pairs={{0,8},{8,16},{16,24},{24,32},{32,40},{40,48},{48,56},{56,64},{64,7... | collective-permute-start | bytes 3145736 | tf_op jit(solution)/shard_map/ppermute | solution.py:43
  8.1 36.2 %collective-permute-start.1 = (f32[256,8,128]{2,1,0:T(8,128)S(1)}, f32[256,8,128]{2,1,0:T(8,128)S(1)}, u32[]{:S(2)}, u32[]{:S(2)}) collective-permute-start(f32[256,8,128]{2,1,0:T(8,128)S(1)} %get-tuple-element.31.refs_1_.mid_ref), channel_id=1, source_target_pairs={{0,120},{8,0},{16,8},{24,16},{32,24},{40,32},{48,40},{56,48},{64,5... | collective-permute-start | bytes 3145736 | tf_op jit(solution)/shard_map/ppermute | solution.py:44
  15.2 4.7 %collective-permute-start.7 = (f32[64,8,128]{2,1,0:T(8,128)S(1)}, f32[64,8,128]{2,1,0:T(8,128)S(1)}, u32[]{:S(2)}, u32[]{:S(2)}) collective-permute-start(f32[64,8,128]{2,1,0:T(8,128)S(1)} %bitcast.10), channel_id=1, source_target_pairs={{0,7},{1,0},{2,1},{3,2},{4,3},{5,4},{6,5},{7,6},{8,15},{9,8},{10,9... | collective-permute-start | bytes 786440 | tf_op jit(solution)/shard_map/ppermute | solution.py:44
  19.9 7.5 %collective-permute-start.2 = (f32[64,8,128]{2,1,0:T(8,128)S(1)}, f32[64,8,128]{2,1,0:T(8,128)S(1)}, u32[]{:S(2)}, u32[]{:S(2)}) collective-permute-start(f32[64,8,128]{2,1,0:T(8,128)S(1)} %bitcast.9), channel_id=1, source_target_pairs={{0,1},{1,2},{2,3},{3,4},{4,5},{5,6},{6,7},{7,0},{8,9},{9,10},{10,1... | collective-permute-start | bytes 786440 | tf_op jit(solution)/shard_map/ppermute | solution.py:43
  21.9 8.3 %collective-permute-start.8 = (f32[64,8,128]{2,1,0:T(8,128)S(1)}, f32[64,8,128]{2,1,0:T(8,128)S(1)}, u32[]{:S(2)}, u32[]{:S(2)}) collective-permute-start(f32[64,8,128]{2,1,0:T(8,128)S(1)} %get-tuple-element.35), channel_id=1, source_target_pairs={{0,1},{1,2},{2,3},{3,4},{4,5},{5,6},{6,7},{7,0},{8,9},{9,10},{10,1... | collective-permute-start | bytes 786440 | tf_op jit(solution)/shard_map/ppermute | solution.py:43
  21.9 12.4 %collective-permute-start.9 = (f32[64,8,128]{2,1,0:T(8,128)S(1)}, f32[64,8,128]{2,1,0:T(8,128)S(1)}, u32[]{:S(2)}, u32[]{:S(2)}) collective-permute-start(f32[64,8,128]{2,1,0:T(8,128)S(1)} %get-tuple-element.36), channel_id=1, source_target_pairs={{0,7},{1,0},{2,1},{3,2},{4,3},{5,4},{6,5},{7,6},{8,15},{9,8},{10,9... | collective-permute-start | bytes 786440 | tf_op jit(solution)/shard_map/ppermute | solution.py:44
  27.4 27.6 %collective-permute-start.10 = (f32[128,8,128]{2,1,0:T(8,128)S(1)}, f32[128,8,128]{2,1,0:T(8,128)S(1)}, u32[]{:S(2)}, u32[]{:S(2)}) collective-permute-start(f32[128,8,128]{2,1,0:T(8,128)S(1)} %get-tuple-element.41.refs_1_.mid_ref), channel_id=1, source_target_pairs={{0,8},{8,16},{16,24},{24,32},{32,40},{40,48},{48,56},{56,64},{64,7... | collective-permute-start | bytes 1572872 | tf_op jit(solution)/shard_map/ppermute | solution.py:43
  30.2 24.8 %collective-permute-start.11 = (f32[128,8,128]{2,1,0:T(8,128)S(1)}, f32[128,8,128]{2,1,0:T(8,128)S(1)}, u32[]{:S(2)}, u32[]{:S(2)}) collective-permute-start(f32[128,8,128]{2,1,0:T(8,128)S(1)} %get-tuple-element.41.refs_1_.mid_ref), channel_id=1, source_target_pairs={{0,120},{8,0},{16,8},{24,16},{32,24},{40,32},{48,40},{56,48},{64,5... | collective-permute-start | bytes 1572872 | tf_op jit(solution)/shard_map/ppermute | solution.py:44
  34.3 4.8 %collective-permute-start.3 = (f32[64,8,128]{2,1,0:T(8,128)S(1)}, f32[64,8,128]{2,1,0:T(8,128)S(1)}, u32[]{:S(2)}, u32[]{:S(2)}) collective-permute-start(f32[64,8,128]{2,1,0:T(8,128)S(1)} %bitcast.8), channel_id=1, source_target_pairs={{0,7},{1,0},{2,1},{3,2},{4,3},{5,4},{6,5},{7,6},{8,15},{9,8},{10,9... | collective-permute-start | bytes 786440 | tf_op jit(solution)/shard_map/ppermute | solution.py:44
  44.3 6.3 %collective-permute-start.12 = (f32[48,8,128]{2,1,0:T(8,128)S(1)}, f32[48,8,128]{2,1,0:T(8,128)S(1)}, u32[]{:S(2)}, u32[]{:S(2)}) collective-permute-start(f32[48,8,128]{2,1,0:T(8,128)S(1)} %get-tuple-element.44), channel_id=1, source_target_pairs={{0,1},{1,2},{2,3},{3,4},{4,5},{5,6},{6,7},{7,0},{8,9},{9,10},{10,1... | collective-permute-start | bytes 589832 | tf_op jit(solution)/shard_map/ppermute | solution.py:43
  44.3 6.3 %collective-permute-start.13 = (f32[48,8,128]{2,1,0:T(8,128)S(1)}, f32[48,8,128]{2,1,0:T(8,128)S(1)}, u32[]{:S(2)}, u32[]{:S(2)}) collective-permute-start(f32[48,8,128]{2,1,0:T(8,128)S(1)} %get-tuple-element.45), channel_id=1, source_target_pairs={{0,7},{1,0},{2,1},{3,2},{4,3},{5,4},{6,5},{7,6},{8,15},{9,8},{10,9... | collective-permute-start | bytes 589832 | tf_op jit(solution)/shard_map/ppermute | solution.py:44
  47.4 11.8 %collective-permute-start.14 = (f32[112,8,128]{2,1,0:T(8,128)S(1)}, f32[112,8,128]{2,1,0:T(8,128)S(1)}, u32[]{:S(2)}, u32[]{:S(2)}) collective-permute-start(f32[112,8,128]{2,1,0:T(8,128)S(1)} %get-tuple-element.50), channel_id=1, source_target_pairs={{0,1},{1,2},{2,3},{3,4},{4,5},{5,6},{6,7},{7,0},{8,9},{9,10},{10,1... | collective-permute-start | bytes 1376264 | tf_op jit(solution)/shard_map/ppermute | solution.py:43
  50.6 8.5 %collective-permute-start.15 = (f32[112,8,128]{2,1,0:T(8,128)S(1)}, f32[112,8,128]{2,1,0:T(8,128)S(1)}, u32[]{:S(2)}, u32[]{:S(2)}) collective-permute-start(f32[112,8,128]{2,1,0:T(8,128)S(1)} %get-tuple-element.51), channel_id=1, source_target_pairs={{0,7},{1,0},{2,1},{3,2},{4,3},{5,4},{6,5},{7,6},{8,15},{9,8},{10,9... | collective-permute-start | bytes 1376264 | tf_op jit(solution)/shard_map/ppermute | solution.py:44
  55.1 9.8 %collective-permute-start.16 = (f32[112,8,128]{2,1,0:T(8,128)S(1)}, f32[112,8,128]{2,1,0:T(8,128)S(1)}, u32[]{:S(2)}, u32[]{:S(2)}) collective-permute-start(f32[112,8,128]{2,1,0:T(8,128)S(1)} %get-tuple-element.54), channel_id=1, source_target_pairs={{0,1},{1,2},{2,3},{3,4},{4,5},{5,6},{6,7},{7,0},{8,9},{9,10},{10,1... | collective-permute-start | bytes 1376264 | tf_op jit(solution)/shard_map/ppermute | solution.py:43
  56.3 8.6 %collective-permute-start.17 = (f32[112,8,128]{2,1,0:T(8,128)S(1)}, f32[112,8,128]{2,1,0:T(8,128)S(1)}, u32[]{:S(2)}, u32[]{:S(2)}) collective-permute-start(f32[112,8,128]{2,1,0:T(8,128)S(1)} %get-tuple-element.55), channel_id=1, source_target_pairs={{0,7},{1,0},{2,1},{3,2},{4,3},{5,4},{6,5},{7,6},{8,15},{9,8},{10,9... | collective-permute-start | bytes 1376264 | tf_op jit(solution)/shard_map/ppermute | solution.py:44
  70.7 1.2 %collective-permute-start.18 = (f32[8,128]{1,0:T(8,128)S(1)}, f32[8,128]{1,0:T(8,128)S(1)}, u32[]{:S(2)}, u32[]{:S(2)}) collective-permute-start(f32[8,128]{1,0:T(8,128)S(1)} %gram_rows.7), channel_id=1, source_target_pairs={{0,1},{1,0},{2,3},{3,2},{4,5},{5,4},{6,7},{7,6},{8,9},{9,8},{10,11... | collective-permute-start | bytes 12296 | tf_op jit(solution)/shard_map/ppermute | solution.py:505

commit v3 on v2

--- a/solution.py
+++ b/solution.py
@@ -14,8 +14,9 @@
 HALF_W = 4.0
 NEAR = (2.0 / HALF_W) * -0.5 * (4.0 / 3.0)
 FAR = (2.0 / HALF_W) * 0.5 / 12.0
-DIAG_SCALE = 2.0 / HALF_W
-DIAG_SHIFT = (2.0 / HALF_W) * (3 * 0.5 * 2.5 - CENTER)
+DIAG_SCALE = (2.0 / HALF_W) / FAR
+DIAG_SHIFT = (2.0 / HALF_W) * (3 * 0.5 * 2.5 - CENTER) / FAR
+BACK = (2.0 / FAR**2, 1.0 / FAR**2, 1.0 / FAR**2)
 
 GROUP = 8
 PREP_VMEM = 59 * 2**20
@@ -241,12 +242,13 @@
             near = (column[1:-3] + column[3:-1]) + (source(plane - 1, first, last) + source(plane + 1, first, last))
             far = (column[:-4] + column[4:]) + (source(plane - 2, first, last) + source(plane + 2, first, last))
             diag = diag_ref[plane, first:last][:, None, :]
-            applied = diag * center + FAR * ((z_part(center, matrix) + far) - 16.0 * near)
-            fresh = 0.5 * applied if step == 0 else applied - chain[step - 1](plane, first, last)
+            fresh = diag * center + ((z_part(center, matrix) + far) - 16.0 * near)
+            if step > 0:
+                fresh = fresh - BACK[step - 1] * chain[step - 1](plane, first, last)
             if step < DEG - 1:
                 steps[step][plane, first:last] = fresh
             else:
-                out_ref[:, plane - HALO] = jnp.swapaxes(fresh, 0, 1)
+                out_ref[:, plane - HALO] = jnp.swapaxes((0.5 * FAR**DEG) * fresh, 0, 1)
 
 
 def filter_kernel(unit, chunk_groups, own_at, cx, cy, lo_ref, mid_ref, hi_ref, yl_ref, yh_ref, *refs):

time: 96.9 us -> 96.4 us (level)
  Pallas kernels: 27.8 us -> 25.6 us
    pallas_call x4, Pallas kernels: 17.5 us -> 15.2 us  [run_filter(): pl.pallas_call(functools.partial(filter_kernel, unit, chunk_groups, own_a...]
  transfers between devices with their start and end apart: 19 -> 19, of which waited for: 8 -> 10; matrix products, arithmetic and copies ran while one was open for 0% -> 0% of each run, Pallas kernels for 17% -> 15%
where the time goes in v3:
time: 96.4 us; the launch traced here: 96.2 us
  starting transfers between devices  26.6 us (28%)
  Pallas kernels  25.6 us (27%)
  waiting for transfers between devices  22 us (23%)
  blocking collectives  21.3 us (22%)
    ppermute x9, starting transfers between devices, both_ways(): lax.ppermute(low_part, axis, shift_perm(axis, -1))  22 us
    all_to_all x1, blocking collectives, body(): received = lax.all_to_all(chip, ('gx', 'gz'), 0, 0, tiled=True)  21.3 us
    ppermute x9, waiting for transfers between devices, both_ways(): lax.ppermute(high_part, axis, shift_perm(axis, 1))  17.4 us
    pallas_call x4, Pallas kernels, run_filter(): pl.pallas_call(functools.partial(filter_kernel, unit, chunk_groups, own_a...  15.2 us
    pallas_call x4, Pallas kernels, run_gram(): pl.pallas_call(functools.partial(gram_kernel, offset, scale, counts), out...  4.01 us
    pallas_call x1, Pallas kernels, run_solve(): pl.pallas_call(functools.partial(solve_kernel, counts), out_shape=jax.Sha...  3.88 us
    ppermute x9, starting transfers between devices, both_ways(): lax.ppermute(high_part, axis, shift_perm(axis, 1))  3.85 us
    ppermute x9, waiting for transfers between devices, both_ways(): lax.ppermute(low_part, axis, shift_perm(axis, -1))  3.85 us
  transfers between devices with their start and end apart: 19, of which 10 were waited for; matrix products, arithmetic and copies ran while one was open for 0% of the time, Pallas kernels for 15%

profile of v3, /device:TPU:0, one launch (start us, length us, event | category | flops | bytes accessed | tf_op | source)
XLA Modules:
  0.0 96.2 jit_solution(14886928325592452114)
XLA Ops:
  0.0 2.0 %first_tiles.1 = f32[144,8,128]{2,1,0:T(8,128)} custom-call(f32[8,16,128]{2,1,0:T(8,128)} %pot_ref.3, f32[32,8,16,128]{3,2,1,0:T(8,128)} %orb_ref.3), custom_call_target="tpu_custom_call" | custom-call | tf_op jit(solution)/shard_map/first_tiles/pallas_call | solution.py:112
  2.0 1.6 %collective-permute-start.4 = (f32[144,8,128]{2,1,0:T(8,128)}, f32[144,8,128]{2,1,0:T(8,128)S(1)}, u32[]{:S(2)}, u32[]{:S(2)}) collective-permute-start(f32[144,8,128]{2,1,0:T(8,128)} %first_tiles.1), channel_id=1, source_target_pairs={{0,8},{8,16},{16,24},{24,32},{32,40},{40,48},{48,56},{56,64},{64,7... | collective-permute-start | bytes 1769480 | tf_op jit(solution)/shard_map/ppermute | solution.py:44
  3.7 3.8 %collective-permute-start.5 = (f32[144,8,128]{2,1,0:T(8,128)}, f32[144,8,128]{2,1,0:T(8,128)S(1)}, u32[]{:S(2)}, u32[]{:S(2)}) collective-permute-start(f32[144,8,128]{2,1,0:T(8,128)} %first_tiles.1), channel_id=1, source_target_pairs={{0,120},{8,0},{16,8},{24,16},{32,24},{40,32},{48,40},{56,48},{64,5... | collective-permute-start | bytes 1769480 | tf_op jit(solution)/shard_map/ppermute | solution.py:45
  7.5 0.4 all_tiles.1
  8.1 5.3 %collective-permute-start.1 = (f32[256,8,128]{2,1,0:T(8,128)S(1)}, f32[256,8,128]{2,1,0:T(8,128)S(1)}, u32[]{:S(2)}, u32[]{:S(2)}) collective-permute-start(f32[256,8,128]{2,1,0:T(8,128)S(1)} %get-tuple-element.31.refs_1_.mid_ref), channel_id=1, source_target_pairs={{0,120},{8,0},{16,8},{24,16},{32,24},{40,32},{48,40},{56,48},{64,5... | collective-permute-start | bytes 3145736 | tf_op jit(solution)/shard_map/ppermute | solution.py:45
  13.4 1.8 %collective-permute-done.6.refs_0_ = f32[64,8,128]{2,1,0:T(8,128)S(1)} collective-permute-done((f32[64,8,128]{2,1,0:T(8,128)S(1)}, f32[64,8,128]{2,1,0:T(8,128)S(1)}, u32[]{:S(2)}, u32[]{:S(2)}) %collective-permute-start.6) | collective-permute-done | bytes 262176 | tf_op jit(solution)/shard_map/ppermute | solution.py:44
  15.2 0.8 collective-permute-start.7
  16.1 3.8 %collective-permute-done.7.refs_1_ = f32[64,8,128]{2,1,0:T(8,128)S(1)} collective-permute-done((f32[64,8,128]{2,1,0:T(8,128)S(1)}, f32[64,8,128]{2,1,0:T(8,128)S(1)}, u32[]{:S(2)}, u32[]{:S(2)}) %collective-permute-start.7) | collective-permute-done | bytes 262176 | tf_op jit(solution)/shard_map/ppermute | solution.py:45
  19.9 1.0 %collective-permute-start.2 = (f32[64,8,128]{2,1,0:T(8,128)S(1)}, f32[64,8,128]{2,1,0:T(8,128)S(1)}, u32[]{:S(2)}, u32[]{:S(2)}) collective-permute-start(f32[64,8,128]{2,1,0:T(8,128)S(1)} %bitcast.9), channel_id=1, source_target_pairs={{0,1},{1,2},{2,3},{3,4},{4,5},{5,6},{6,7},{7,0},{8,9},{9,10},{10,1... | collective-permute-start | bytes 786440 | tf_op jit(solution)/shard_map/ppermute | solution.py:44
  20.9 0.9 collective-permute-done.4.refs_0_.lo_ref
  21.9 2.9 %collective-permute-start.9 = (f32[64,8,128]{2,1,0:T(8,128)S(1)}, f32[64,8,128]{2,1,0:T(8,128)S(1)}, u32[]{:S(2)}, u32[]{:S(2)}) collective-permute-start(f32[64,8,128]{2,1,0:T(8,128)S(1)} %get-tuple-element.36), channel_id=1, source_target_pairs={{0,7},{1,0},{2,1},{3,2},{4,3},{5,4},{6,5},{7,6},{8,15},{9,8},{10,9... | collective-permute-start | bytes 786440 | tf_op jit(solution)/shard_map/ppermute | solution.py:45
  24.8 2.6 %collective-permute-done.2.refs_0_ = f32[64,8,128]{2,1,0:T(8,128)S(1)} collective-permute-done((f32[64,8,128]{2,1,0:T(8,128)S(1)}, f32[64,8,128]{2,1,0:T(8,128)S(1)}, u32[]{:S(2)}, u32[]{:S(2)}) %collective-permute-start.2) | collective-permute-done | bytes 262176 | tf_op jit(solution)/shard_map/ppermute | solution.py:44
  27.4 2.8 %collective-permute-done.8.yl_ref = f32[64,8,128]{2,1,0:T(8,128)S(1)} collective-permute-done((f32[64,8,128]{2,1,0:T(8,128)S(1)}, f32[64,8,128]{2,1,0:T(8,128)S(1)}, u32[]{:S(2)}, u32[]{:S(2)}) %collective-permute-start.8) | collective-permute-done | bytes 262176 | tf_op jit(solution)/shard_map/ppermute | solution.py:44
  30.2 4.1 %collective-permute-start.11 = (f32[128,8,128]{2,1,0:T(8,128)S(1)}, f32[128,8,128]{2,1,0:T(8,128)S(1)}, u32[]{:S(2)}, u32[]{:S(2)}) collective-permute-start(f32[128,8,128]{2,1,0:T(8,128)S(1)} %get-tuple-element.41.refs_1_.mid_ref), channel_id=1, source_target_pairs={{0,120},{8,0},{16,8},{24,16},{32,24},{40,32},{48,40},{56,48},{64,5... | collective-permute-start | bytes 1572872 | tf_op jit(solution)/shard_map/ppermute | solution.py:45
  34.3 3.8 %filter_orbitals.4 = (f32[8,8,16,128]{3,2,1,0:T(8,128)S(1)}, f32[24,32,128]{2,1,0:T(8,128)S(1)}) custom-call(f32[144,8,128]{2,1,0:T(8,128)S(1)} %collective-permute-done.4.refs_0_.lo_ref, f32[144,8,128]{2,1,0:T(8,128)S(1)} %get-tuple-element.32.refs_1_.mid_ref, f32[144,8,128]{2,1,0:T(8,128)S(1)} %collective-permute-done.5.refs_2_.hi_ref, ...), custom_call_target="tpu_custom_call" | custom-call | bytes 100 | tf_op jit(solution)/shard_map/filter_orbitals/pallas_call | solution.py:307
  38.1 0.5 gram_rows.4.refs_4_
  38.6 5.7 %collective-permute-done.refs_0_.lo_ref = f32[256,8,128]{2,1,0:T(8,128)S(1)} collective-permute-done((f32[256,8,128]{2,1,0:T(8,128)S(1)}, f32[256,8,128]{2,1,0:T(8,128)S(1)}, u32[]{:S(2)}, u32[]{:S(2)}) %collective-permute-start) | collective-permute-done | bytes 1048608 | tf_op jit(solution)/shard_map/ppermute | solution.py:44
  44.3 2.9 %collective-permute-start.13 = (f32[48,8,128]{2,1,0:T(8,128)S(1)}, f32[48,8,128]{2,1,0:T(8,128)S(1)}, u32[]{:S(2)}, u32[]{:S(2)}) collective-permute-start(f32[48,8,128]{2,1,0:T(8,128)S(1)} %get-tuple-element.45), channel_id=1, source_target_pairs={{0,7},{1,0},{2,1},{3,2},{4,3},{5,4},{6,5},{7,6},{8,15},{9,8},{10,9... | collective-permute-start | bytes 589832 | tf_op jit(solution)/shard_map/ppermute | solution.py:45
  47.4 3.3 %collective-permute-done.12.yl_ref = f32[48,8,128]{2,1,0:T(8,128)S(1)} collective-permute-done((f32[48,8,128]{2,1,0:T(8,128)S(1)}, f32[48,8,128]{2,1,0:T(8,128)S(1)}, u32[]{:S(2)}, u32[]{:S(2)}) %collective-permute-start.12) | collective-permute-done | bytes 196640 | tf_op jit(solution)/shard_map/ppermute | solution.py:44
  50.6 3.8 %filter_orbitals.5.refs_1_ = f32[8,8,16,128]{3,2,1,0:T(8,128)S(1)} custom-call(f32[256,8,128]{2,1,0:T(8,128)S(1)} %collective-permute-done.refs_0_.lo_ref, f32[256,8,128]{2,1,0:T(8,128)S(1)} %get-tuple-element.31.refs_1_.mid_ref, f32[256,8,128]{2,1,0:T(8,128)S(1)} %collective-permute-done.1.refs_2_.hi_ref, f32[48,8,128]{2,1,0:T(8,128)S(1)} %collective-permute-done.12.yl_ref, ...), custom_call_target="tpu_custom_call" | custom-call | bytes 100 | tf_op jit(solution)/shard_map/filter_orbitals/pallas_call | solution.py:307
  54.4 0.2 collective-permute-done.10.refs_0_.lo_ref
  54.7 1.0 %collective-permute-start.16 = (f32[112,8,128]{2,1,0:T(8,128)S(1)}, f32[112,8,128]{2,1,0:T(8,128)S(1)}, u32[]{:S(2)}, u32[]{:S(2)}) collective-permute-start(f32[112,8,128]{2,1,0:T(8,128)S(1)} %get-tuple-element.54), channel_id=1, source_target_pairs={{0,1},{1,2},{2,3},{3,4},{4,5},{5,6},{6,7},{7,0},{8,9},{9,10},{10,1... | collective-permute-start | bytes 1376264 | tf_op jit(solution)/shard_map/ppermute | solution.py:44
  55.8 2.1 %collective-permute-start.17 = (f32[112,8,128]{2,1,0:T(8,128)S(1)}, f32[112,8,128]{2,1,0:T(8,128)S(1)}, u32[]{:S(2)}, u32[]{:S(2)}) collective-permute-start(f32[112,8,128]{2,1,0:T(8,128)S(1)} %get-tuple-element.55), channel_id=1, source_target_pairs={{0,7},{1,0},{2,1},{3,2},{4,3},{5,4},{6,5},{7,6},{8,15},{9,8},{10,9... | collective-permute-start | bytes 1376264 | tf_op jit(solution)/shard_map/ppermute | solution.py:45
  57.8 0.8 gram_rows.5.refs_5_
  58.7 3.8 %filter_orbitals.6.refs_2_ = f32[8,8,16,128]{3,2,1,0:T(8,128)S(1)} custom-call(f32[256,8,128]{2,1,0:T(8,128)S(1)} %collective-permute-done.refs_0_.lo_ref, f32[256,8,128]{2,1,0:T(8,128)S(1)} %get-tuple-element.31.refs_1_.mid_ref, f32[256,8,128]{2,1,0:T(8,128)S(1)} %collective-permute-done.1.refs_2_.hi_ref, ...), custom_call_target="tpu_custom_call" | custom-call | bytes 100 | tf_op jit(solution)/shard_map/filter_orbitals/pallas_call | solution.py:307
  62.5 1.3 %gram_rows.6.refs_6_ = f32[8,128]{1,0:T(8,128)S(1)} custom-call(f32[8,8,16,128]{3,2,1,0:T(8,128)S(1)} %get-tuple-element.40.refs_0_, f32[8,8,16,128]{3,2,1,0:T(8,128)S(1)} %filter_orbitals.5.refs_1_, f32[8,8,16,128]{3,2,1,0:T(8,128)S(1)} %filter_orbitals.6.refs_2_), custom_call_target="tpu_custom_call" | custom-call | bytes 100 | tf_op jit(solution)/shard_map/gram_rows/pallas_call | solution.py:375
  64.0 3.8 %filter_orbitals.7.refs_3_ = f32[8,8,16,128]{3,2,1,0:T(8,128)S(1)} custom-call(f32[128,8,128]{2,1,0:T(8,128)S(1)} %collective-permute-done.10.refs_0_.lo_ref, f32[128,8,128]{2,1,0:T(8,128)S(1)} %get-tuple-element.41.refs_1_.mid_ref, f32[128,8,128]{2,1,0:T(8,128)S(1)} %collective-permute-done.11.refs_2_.hi_ref, ...), custom_call_target="tpu_custom_call" | custom-call | bytes 100 | tf_op jit(solution)/shard_map/filter_orbitals/pallas_call | solution.py:307
  67.8 1.4 %gram_rows.7 = f32[8,128]{1,0:T(8,128)S(1)} custom-call(f32[8,8,16,128]{3,2,1,0:T(8,128)S(1)} %get-tuple-element.40.refs_0_, f32[8,8,16,128]{3,2,1,0:T(8,128)S(1)} %filter_orbitals.5.refs_1_, f32[8,8,16,128]{3,2,1,0:T(8,128)S(1)} %filter_orbitals.6.refs_2_, f32[8,8,16,128]{3,2,1,0:T(8,128)S(1)} %filter_orbitals.7.refs_3_, f32[8,128]{1,0:T(8,128)S(1)} %gram_rows.4.refs_4_, ...), custom_call_target="tpu_custom_call" | custom-call | bytes 100 | tf_op jit(solution)/shard_map/gram_rows/pallas_call | solution.py:375
  69.2 0.8 collective-permute-start.18
  70.0 0.8 collective-permute-done.18
  70.8 21.3 %all_to_all.5.recv_ref = f32[64,8,128]{2,1,0:T(8,128)S(1)} all-to-all(f32[64,8,128]{2,1,0:T(8,128)S(1)} %broadcast_in_dim.2), channel_id=1, replica_groups=mesh['gx'=16,'gz'=4,'core'=2] {'gx','gz'}, dimensions={0} | all-to-all | bytes 524288 | tf_op jit(solution)/shard_map/all_to_all | solution.py:509
  92.1 3.9 %orthonormalize.1 = f32[32,8,16,128]{3,2,1,0:T(8,128)} custom-call(f32[64,8,128]{2,1,0:T(8,128)S(1)} %all_to_all.5.recv_ref, f32[8,8,16,128]{3,2,1,0:T(8,128)S(1)} %get-tuple-element.40.refs_0_, f32[8,8,16,128]{3,2,1,0:T(8,128)S(1)} %filter_orbitals.5.refs_1_, f32[8,8,16,128]{3,2,1,0:T(8,128)S(1)} %filter_orbitals.6.refs_2_, ...), custom_call_target="tpu_custom_call" | custom-call | tf_op jit(solution)/shard_map/orthonormalize/pallas_call | solution.py:441
  (32 shorter events, 0.7 us)
Async XLA Ops:
  0.0 7.5 %copy-start = (f32[32,8,16,128]{3,2,1,0:T(8,128)S(1)}, f32[32,8,16,128]{3,2,1,0:T(8,128)}, u32[]{:S(2)}) copy-start(f32[32,8,16,128]{3,2,1,0:T(8,128)} %orb_ref.3) | copy-start | bytes 6291460
  0.0 7.5 %copy-start.1 = (f32[8,16,128]{2,1,0:T(8,128)S(1)}, f32[8,16,128]{2,1,0:T(8,128)}, u32[]{:S(2)}) copy-start(f32[8,16,128]{2,1,0:T(8,128)} %pot_ref.3) | copy-start | bytes 196612
  2.0 19.8 %collective-permute-start.4 = (f32[144,8,128]{2,1,0:T(8,128)}, f32[144,8,128]{2,1,0:T(8,128)S(1)}, u32[]{:S(2)}, u32[]{:S(2)}) collective-permute-start(f32[144,8,128]{2,1,0:T(8,128)} %first_tiles.1), channel_id=1, source_target_pairs={{0,8},{8,16},{16,24},{24,32},{32,40},{40,48},{48,56},{56,64},{64,7... | collective-permute-start | bytes 1769480 | tf_op jit(solution)/shard_map/ppermute | solution.py:44
  3.7 18.1 %collective-permute-start.5 = (f32[144,8,128]{2,1,0:T(8,128)}, f32[144,8,128]{2,1,0:T(8,128)S(1)}, u32[]{:S(2)}, u32[]{:S(2)}) collective-permute-start(f32[144,8,128]{2,1,0:T(8,128)} %first_tiles.1), channel_id=1, source_target_pairs={{0,120},{8,0},{16,8},{24,16},{32,24},{40,32},{48,40},{56,48},{64,5... | collective-permute-start | bytes 1769480 | tf_op jit(solution)/shard_map/ppermute | solution.py:45
  8.0 7.3 %collective-permute-start.6 = (f32[64,8,128]{2,1,0:T(8,128)S(1)}, f32[64,8,128]{2,1,0:T(8,128)S(1)}, u32[]{:S(2)}, u32[]{:S(2)}) collective-permute-start(f32[64,8,128]{2,1,0:T(8,128)S(1)} %bitcast.11), channel_id=1, source_target_pairs={{0,1},{1,2},{2,3},{3,4},{4,5},{5,6},{6,7},{7,0},{8,9},{9,10},{10,1... | collective-permute-start | bytes 786440 | tf_op jit(solution)/shard_map/ppermute | solution.py:44
  8.0 36.3 %collective-permute-start = (f32[256,8,128]{2,1,0:T(8,128)S(1)}, f32[256,8,128]{2,1,0:T(8,128)S(1)}, u32[]{:S(2)}, u32[]{:S(2)}) collective-permute-start(f32[256,8,128]{2,1,0:T(8,128)S(1)} %get-tuple-element.31.refs_1_.mid_ref), channel_id=1, source_target_pairs={{0,8},{8,16},{16,24},{24,32},{32,40},{40,48},{48,56},{56,64},{64,7... | collective-permute-start | bytes 3145736 | tf_op jit(solution)/shard_map/ppermute | solution.py:44
  8.1 36.2 %collective-permute-start.1 = (f32[256,8,128]{2,1,0:T(8,128)S(1)}, f32[256,8,128]{2,1,0:T(8,128)S(1)}, u32[]{:S(2)}, u32[]{:S(2)}) collective-permute-start(f32[256,8,128]{2,1,0:T(8,128)S(1)} %get-tuple-element.31.refs_1_.mid_ref), channel_id=1, source_target_pairs={{0,120},{8,0},{16,8},{24,16},{32,24},{40,32},{48,40},{56,48},{64,5... | collective-permute-start | bytes 3145736 | tf_op jit(solution)/shard_map/ppermute | solution.py:45
  15.2 4.7 %collective-permute-start.7 = (f32[64,8,128]{2,1,0:T(8,128)S(1)}, f32[64,8,128]{2,1,0:T(8,128)S(1)}, u32[]{:S(2)}, u32[]{:S(2)}) collective-permute-start(f32[64,8,128]{2,1,0:T(8,128)S(1)} %bitcast.10), channel_id=1, source_target_pairs={{0,7},{1,0},{2,1},{3,2},{4,3},{5,4},{6,5},{7,6},{8,15},{9,8},{10,9... | collective-permute-start | bytes 786440 | tf_op jit(solution)/shard_map/ppermute | solution.py:45
  19.9 7.5 %collective-permute-start.2 = (f32[64,8,128]{2,1,0:T(8,128)S(1)}, f32[64,8,128]{2,1,0:T(8,128)S(1)}, u32[]{:S(2)}, u32[]{:S(2)}) collective-permute-start(f32[64,8,128]{2,1,0:T(8,128)S(1)} %bitcast.9), channel_id=1, source_target_pairs={{0,1},{1,2},{2,3},{3,4},{4,5},{5,6},{6,7},{7,0},{8,9},{9,10},{10,1... | collective-permute-start | bytes 786440 | tf_op jit(solution)/shard_map/ppermute | solution.py:44
  21.9 8.3 %collective-permute-start.8 = (f32[64,8,128]{2,1,0:T(8,128)S(1)}, f32[64,8,128]{2,1,0:T(8,128)S(1)}, u32[]{:S(2)}, u32[]{:S(2)}) collective-permute-start(f32[64,8,128]{2,1,0:T(8,128)S(1)} %get-tuple-element.35), channel_id=1, source_target_pairs={{0,1},{1,2},{2,3},{3,4},{4,5},{5,6},{6,7},{7,0},{8,9},{9,10},{10,1... | collective-permute-start | bytes 786440 | tf_op jit(solution)/shard_map/ppermute | solution.py:44
  21.9 12.4 %collective-permute-start.9 = (f32[64,8,128]{2,1,0:T(8,128)S(1)}, f32[64,8,128]{2,1,0:T(8,128)S(1)}, u32[]{:S(2)}, u32[]{:S(2)}) collective-permute-start(f32[64,8,128]{2,1,0:T(8,128)S(1)} %get-tuple-element.36), channel_id=1, source_target_pairs={{0,7},{1,0},{2,1},{3,2},{4,3},{5,4},{6,5},{7,6},{8,15},{9,8},{10,9... | collective-permute-start | bytes 786440 | tf_op jit(solution)/shard_map/ppermute | solution.py:45
  27.4 27.2 %collective-permute-start.10 = (f32[128,8,128]{2,1,0:T(8,128)S(1)}, f32[128,8,128]{2,1,0:T(8,128)S(1)}, u32[]{:S(2)}, u32[]{:S(2)}) collective-permute-start(f32[128,8,128]{2,1,0:T(8,128)S(1)} %get-tuple-element.41.refs_1_.mid_ref), channel_id=1, source_target_pairs={{0,8},{8,16},{16,24},{24,32},{32,40},{40,48},{48,56},{56,64},{64,7... | collective-permute-start | bytes 1572872 | tf_op jit(solution)/shard_map/ppermute | solution.py:44
  30.2 24.4 %collective-permute-start.11 = (f32[128,8,128]{2,1,0:T(8,128)S(1)}, f32[128,8,128]{2,1,0:T(8,128)S(1)}, u32[]{:S(2)}, u32[]{:S(2)}) collective-permute-start(f32[128,8,128]{2,1,0:T(8,128)S(1)} %get-tuple-element.41.refs_1_.mid_ref), channel_id=1, source_target_pairs={{0,120},{8,0},{16,8},{24,16},{32,24},{40,32},{48,40},{56,48},{64,5... | collective-permute-start | bytes 1572872 | tf_op jit(solution)/shard_map/ppermute | solution.py:45
  34.3 4.3 %collective-permute-start.3 = (f32[64,8,128]{2,1,0:T(8,128)S(1)}, f32[64,8,128]{2,1,0:T(8,128)S(1)}, u32[]{:S(2)}, u32[]{:S(2)}) collective-permute-start(f32[64,8,128]{2,1,0:T(8,128)S(1)} %bitcast.8), channel_id=1, source_target_pairs={{0,7},{1,0},{2,1},{3,2},{4,3},{5,4},{6,5},{7,6},{8,15},{9,8},{10,9... | collective-permute-start | bytes 786440 | tf_op jit(solution)/shard_map/ppermute | solution.py:45
  44.3 6.3 %collective-permute-start.12 = (f32[48,8,128]{2,1,0:T(8,128)S(1)}, f32[48,8,128]{2,1,0:T(8,128)S(1)}, u32[]{:S(2)}, u32[]{:S(2)}) collective-permute-start(f32[48,8,128]{2,1,0:T(8,128)S(1)} %get-tuple-element.44), channel_id=1, source_target_pairs={{0,1},{1,2},{2,3},{3,4},{4,5},{5,6},{6,7},{7,0},{8,9},{9,10},{10,1... | collective-permute-start | bytes 589832 | tf_op jit(solution)/shard_map/ppermute | solution.py:44
  44.3 6.3 %collective-permute-start.13 = (f32[48,8,128]{2,1,0:T(8,128)S(1)}, f32[48,8,128]{2,1,0:T(8,128)S(1)}, u32[]{:S(2)}, u32[]{:S(2)}) collective-permute-start(f32[48,8,128]{2,1,0:T(8,128)S(1)} %get-tuple-element.45), channel_id=1, source_target_pairs={{0,7},{1,0},{2,1},{3,2},{4,3},{5,4},{6,5},{7,6},{8,15},{9,8},{10,9... | collective-permute-start | bytes 589832 | tf_op jit(solution)/shard_map/ppermute | solution.py:45
  47.4 11.3 %collective-permute-start.14 = (f32[112,8,128]{2,1,0:T(8,128)S(1)}, f32[112,8,128]{2,1,0:T(8,128)S(1)}, u32[]{:S(2)}, u32[]{:S(2)}) collective-permute-start(f32[112,8,128]{2,1,0:T(8,128)S(1)} %get-tuple-element.50), channel_id=1, source_target_pairs={{0,1},{1,2},{2,3},{3,4},{4,5},{5,6},{6,7},{7,0},{8,9},{9,10},{10,1... | collective-permute-start | bytes 1376264 | tf_op jit(solution)/shard_map/ppermute | solution.py:44
  50.6 8.0 %collective-permute-start.15 = (f32[112,8,128]{2,1,0:T(8,128)S(1)}, f32[112,8,128]{2,1,0:T(8,128)S(1)}, u32[]{:S(2)}, u32[]{:S(2)}) collective-permute-start(f32[112,8,128]{2,1,0:T(8,128)S(1)} %get-tuple-element.51), channel_id=1, source_target_pairs={{0,7},{1,0},{2,1},{3,2},{4,3},{5,4},{6,5},{7,6},{8,15},{9,8},{10,9... | collective-permute-start | bytes 1376264 | tf_op jit(solution)/shard_map/ppermute | solution.py:45
  54.7 9.3 %collective-permute-start.16 = (f32[112,8,128]{2,1,0:T(8,128)S(1)}, f32[112,8,128]{2,1,0:T(8,128)S(1)}, u32[]{:S(2)}, u32[]{:S(2)}) collective-permute-start(f32[112,8,128]{2,1,0:T(8,128)S(1)} %get-tuple-element.54), channel_id=1, source_target_pairs={{0,1},{1,2},{2,3},{3,4},{4,5},{5,6},{6,7},{7,0},{8,9},{9,10},{10,1... | collective-permute-start | bytes 1376264 | tf_op jit(solution)/shard_map/ppermute | solution.py:44
  55.8 8.2 %collective-permute-start.17 = (f32[112,8,128]{2,1,0:T(8,128)S(1)}, f32[112,8,128]{2,1,0:T(8,128)S(1)}, u32[]{:S(2)}, u32[]{:S(2)}) collective-permute-start(f32[112,8,128]{2,1,0:T(8,128)S(1)} %get-tuple-element.55), channel_id=1, source_target_pairs={{0,7},{1,0},{2,1},{3,2},{4,3},{5,4},{6,5},{7,6},{8,15},{9,8},{10,9... | collective-permute-start | bytes 1376264 | tf_op jit(solution)/shard_map/ppermute | solution.py:45
  69.2 1.6 %collective-permute-start.18 = (f32[8,128]{1,0:T(8,128)S(1)}, f32[8,128]{1,0:T(8,128)S(1)}, u32[]{:S(2)}, u32[]{:S(2)}) collective-permute-start(f32[8,128]{1,0:T(8,128)S(1)} %gram_rows.7), channel_id=1, source_target_pairs={{0,1},{1,0},{2,3},{3,2},{4,5},{5,4},{6,7},{7,6},{8,9},{9,8},{10,11... | collective-permute-start | bytes 12296 | tf_op jit(solution)/shard_map/ppermute | solution.py:507

commit v4 on v3

--- a/solution.py
+++ b/solution.py
@@ -215,10 +215,10 @@
     middle = rest.astype(jnp.bfloat16)
     low = (rest - middle.astype(jnp.float32)).astype(jnp.bfloat16)
 
-    def times(part):
-        return jnp.dot(part, matrix, preferred_element_type=jnp.float32)
-
-    return (times(high) + (times(middle) + times(low))).reshape(center.shape)
+    both = jnp.concatenate([high, middle], axis=1)
+    twice = jnp.concatenate([matrix, matrix], axis=0)
+    upper = jnp.dot(both, twice, preferred_element_type=jnp.float32)
+    return (upper + jnp.dot(low, matrix, preferred_element_type=jnp.float32)).reshape(center.shape)
 
 
 def four_steps(cx, cy, start, steps, diag_ref, out_ref):

time: 96.4 us -> 96.7 us (level)
  Pallas kernels: 25.6 us -> 27 us
    pallas_call x4, Pallas kernels: 15.2 us -> 16.7 us  [run_filter(): pl.pallas_call(functools.partial(filter_kernel, unit, chunk_groups, own_a...]
  transfers between devices with their start and end apart: 19 -> 19, of which waited for: 10 -> 8; matrix products, arithmetic and copies ran while one was open for 0% -> 0% of each run, Pallas kernels for 15% -> 16%
where the time goes in v4:
time: 96.7 us; the launch traced here: 96.5 us
  Pallas kernels  27 us (28%)
  starting transfers between devices  26.3 us (27%)
  waiting for transfers between devices  21.5 us (22%)
  blocking collectives  21.1 us (22%)
    ppermute x9, starting transfers between devices, both_ways(): lax.ppermute(low_part, axis, shift_perm(axis, -1))  22 us
    all_to_all x1, blocking collectives, body(): received = lax.all_to_all(chip, ('gx', 'gz'), 0, 0, tiled=True)  21.1 us
    pallas_call x4, Pallas kernels, run_filter(): pl.pallas_call(functools.partial(filter_kernel, unit, chunk_groups, own_a...  16.7 us
    ppermute x9, waiting for transfers between devices, both_ways(): lax.ppermute(high_part, axis, shift_perm(axis, 1))  16.7 us
    ppermute x9, starting transfers between devices, both_ways(): lax.ppermute(high_part, axis, shift_perm(axis, 1))  4.01 us
    pallas_call x1, Pallas kernels, run_solve(): pl.pallas_call(functools.partial(solve_kernel, counts), out_shape=jax.Sha...  3.88 us
    ppermute x9, waiting for transfers between devices, both_ways(): lax.ppermute(low_part, axis, shift_perm(axis, -1))  3.85 us
    pallas_call x4, Pallas kernels, run_gram(): pl.pallas_call(functools.partial(gram_kernel, offset, scale, counts), out...  3.79 us
  transfers between devices with their start and end apart: 19, of which 8 were waited for; matrix products, arithmetic and copies ran while one was open for 0% of the time, Pallas kernels for 16%

profile of v4, /device:TPU:0, one launch (start us, length us, event | category | flops | bytes accessed | tf_op | source)
XLA Modules:
  0.0 96.5 jit_solution(12367159383286109633)
XLA Ops:
  0.0 2.0 %first_tiles.1 = f32[144,8,128]{2,1,0:T(8,128)} custom-call(f32[8,16,128]{2,1,0:T(8,128)} %pot_ref.3, f32[32,8,16,128]{3,2,1,0:T(8,128)} %orb_ref.3), custom_call_target="tpu_custom_call" | custom-call | tf_op jit(solution)/shard_map/first_tiles/pallas_call | solution.py:112
  2.0 1.6 %collective-permute-start.4 = (f32[144,8,128]{2,1,0:T(8,128)}, f32[144,8,128]{2,1,0:T(8,128)S(1)}, u32[]{:S(2)}, u32[]{:S(2)}) collective-permute-start(f32[144,8,128]{2,1,0:T(8,128)} %first_tiles.1), channel_id=1, source_target_pairs={{0,8},{8,16},{16,24},{24,32},{32,40},{40,48},{48,56},{56,64},{64,7... | collective-permute-start | bytes 1769480 | tf_op jit(solution)/shard_map/ppermute | solution.py:44
  3.7 3.8 %collective-permute-start.5 = (f32[144,8,128]{2,1,0:T(8,128)}, f32[144,8,128]{2,1,0:T(8,128)S(1)}, u32[]{:S(2)}, u32[]{:S(2)}) collective-permute-start(f32[144,8,128]{2,1,0:T(8,128)} %first_tiles.1), channel_id=1, source_target_pairs={{0,120},{8,0},{16,8},{24,16},{32,24},{40,32},{48,40},{56,48},{64,5... | collective-permute-start | bytes 1769480 | tf_op jit(solution)/shard_map/ppermute | solution.py:45
  7.5 0.4 all_tiles.1
  8.0 0.1 collective-permute-start
  8.1 5.3 %collective-permute-start.1 = (f32[256,8,128]{2,1,0:T(8,128)S(1)}, f32[256,8,128]{2,1,0:T(8,128)S(1)}, u32[]{:S(2)}, u32[]{:S(2)}) collective-permute-start(f32[256,8,128]{2,1,0:T(8,128)S(1)} %get-tuple-element.31.refs_1_.mid_ref), channel_id=1, source_target_pairs={{0,120},{8,0},{16,8},{24,16},{32,24},{40,32},{48,40},{56,48},{64,5... | collective-permute-start | bytes 3145736 | tf_op jit(solution)/shard_map/ppermute | solution.py:45
  13.4 1.8 %collective-permute-done.6.refs_0_ = f32[64,8,128]{2,1,0:T(8,128)S(1)} collective-permute-done((f32[64,8,128]{2,1,0:T(8,128)S(1)}, f32[64,8,128]{2,1,0:T(8,128)S(1)}, u32[]{:S(2)}, u32[]{:S(2)}) %collective-permute-start.6) | collective-permute-done | bytes 262176 | tf_op jit(solution)/shard_map/ppermute | solution.py:44
  15.2 0.8 collective-permute-start.7
  16.1 3.8 %collective-permute-done.7.refs_1_ = f32[64,8,128]{2,1,0:T(8,128)S(1)} collective-permute-done((f32[64,8,128]{2,1,0:T(8,128)S(1)}, f32[64,8,128]{2,1,0:T(8,128)S(1)}, u32[]{:S(2)}, u32[]{:S(2)}) %collective-permute-start.7) | collective-permute-done | bytes 262176 | tf_op jit(solution)/shard_map/ppermute | solution.py:45
  19.9 1.0 %collective-permute-start.2 = (f32[64,8,128]{2,1,0:T(8,128)S(1)}, f32[64,8,128]{2,1,0:T(8,128)S(1)}, u32[]{:S(2)}, u32[]{:S(2)}) collective-permute-start(f32[64,8,128]{2,1,0:T(8,128)S(1)} %bitcast.9), channel_id=1, source_target_pairs={{0,1},{1,2},{2,3},{3,4},{4,5},{5,6},{6,7},{7,0},{8,9},{9,10},{10,1... | collective-permute-start | bytes 786440 | tf_op jit(solution)/shard_map/ppermute | solution.py:44
  20.9 0.9 collective-permute-done.4.refs_0_.lo_ref
  21.9 2.9 %collective-permute-start.9 = (f32[64,8,128]{2,1,0:T(8,128)S(1)}, f32[64,8,128]{2,1,0:T(8,128)S(1)}, u32[]{:S(2)}, u32[]{:S(2)}) collective-permute-start(f32[64,8,128]{2,1,0:T(8,128)S(1)} %get-tuple-element.36), channel_id=1, source_target_pairs={{0,7},{1,0},{2,1},{3,2},{4,3},{5,4},{6,5},{7,6},{8,15},{9,8},{10,9... | collective-permute-start | bytes 786440 | tf_op jit(solution)/shard_map/ppermute | solution.py:45
  24.8 2.6 %collective-permute-done.2.refs_0_ = f32[64,8,128]{2,1,0:T(8,128)S(1)} collective-permute-done((f32[64,8,128]{2,1,0:T(8,128)S(1)}, f32[64,8,128]{2,1,0:T(8,128)S(1)}, u32[]{:S(2)}, u32[]{:S(2)}) %collective-permute-start.2) | collective-permute-done | bytes 262176 | tf_op jit(solution)/shard_map/ppermute | solution.py:44
  27.4 2.8 %collective-permute-done.8.yl_ref = f32[64,8,128]{2,1,0:T(8,128)S(1)} collective-permute-done((f32[64,8,128]{2,1,0:T(8,128)S(1)}, f32[64,8,128]{2,1,0:T(8,128)S(1)}, u32[]{:S(2)}, u32[]{:S(2)}) %collective-permute-start.8) | collective-permute-done | bytes 262176 | tf_op jit(solution)/shard_map/ppermute | solution.py:44
  30.2 4.1 %collective-permute-start.11 = (f32[128,8,128]{2,1,0:T(8,128)S(1)}, f32[128,8,128]{2,1,0:T(8,128)S(1)}, u32[]{:S(2)}, u32[]{:S(2)}) collective-permute-start(f32[128,8,128]{2,1,0:T(8,128)S(1)} %get-tuple-element.41.refs_1_.mid_ref), channel_id=1, source_target_pairs={{0,120},{8,0},{16,8},{24,16},{32,24},{40,32},{48,40},{56,48},{64,5... | collective-permute-start | bytes 1572872 | tf_op jit(solution)/shard_map/ppermute | solution.py:45
  34.3 4.2 %filter_orbitals.4 = (f32[8,8,16,128]{3,2,1,0:T(8,128)S(1)}, f32[24,32,128]{2,1,0:T(8,128)S(1)}) custom-call(f32[144,8,128]{2,1,0:T(8,128)S(1)} %collective-permute-done.4.refs_0_.lo_ref, f32[144,8,128]{2,1,0:T(8,128)S(1)} %get-tuple-element.32.refs_1_.mid_ref, f32[144,8,128]{2,1,0:T(8,128)S(1)} %collective-permute-done.5.refs_2_.hi_ref, ...), custom_call_target="tpu_custom_call" | custom-call | bytes 100 | tf_op jit(solution)/shard_map/filter_orbitals/pallas_call | solution.py:307
  38.4 0.5 gram_rows.4.refs_4_
  38.9 5.3 %collective-permute-done.refs_0_.lo_ref = f32[256,8,128]{2,1,0:T(8,128)S(1)} collective-permute-done((f32[256,8,128]{2,1,0:T(8,128)S(1)}, f32[256,8,128]{2,1,0:T(8,128)S(1)}, u32[]{:S(2)}, u32[]{:S(2)}) %collective-permute-start) | collective-permute-done | bytes 1048608 | tf_op jit(solution)/shard_map/ppermute | solution.py:44
  44.3 2.9 %collective-permute-start.13 = (f32[48,8,128]{2,1,0:T(8,128)S(1)}, f32[48,8,128]{2,1,0:T(8,128)S(1)}, u32[]{:S(2)}, u32[]{:S(2)}) collective-permute-start(f32[48,8,128]{2,1,0:T(8,128)S(1)} %get-tuple-element.45), channel_id=1, source_target_pairs={{0,7},{1,0},{2,1},{3,2},{4,3},{5,4},{6,5},{7,6},{8,15},{9,8},{10,9... | collective-permute-start | bytes 589832 | tf_op jit(solution)/shard_map/ppermute | solution.py:45
  47.4 3.3 %collective-permute-done.12.yl_ref = f32[48,8,128]{2,1,0:T(8,128)S(1)} collective-permute-done((f32[48,8,128]{2,1,0:T(8,128)S(1)}, f32[48,8,128]{2,1,0:T(8,128)S(1)}, u32[]{:S(2)}, u32[]{:S(2)}) %collective-permute-start.12) | collective-permute-done | bytes 196640 | tf_op jit(solution)/shard_map/ppermute | solution.py:44
  50.6 4.1 %filter_orbitals.5.refs_1_ = f32[8,8,16,128]{3,2,1,0:T(8,128)S(1)} custom-call(f32[256,8,128]{2,1,0:T(8,128)S(1)} %collective-permute-done.refs_0_.lo_ref, f32[256,8,128]{2,1,0:T(8,128)S(1)} %get-tuple-element.31.refs_1_.mid_ref, f32[256,8,128]{2,1,0:T(8,128)S(1)} %collective-permute-done.1.refs_2_.hi_ref, f32[48,8,128]{2,1,0:T(8,128)S(1)} %collective-permute-done.12.yl_ref, ...), custom_call_target="tpu_custom_call" | custom-call | bytes 100 | tf_op jit(solution)/shard_map/filter_orbitals/pallas_call | solution.py:307
  54.9 1.2 %collective-permute-start.16 = (f32[112,8,128]{2,1,0:T(8,128)S(1)}, f32[112,8,128]{2,1,0:T(8,128)S(1)}, u32[]{:S(2)}, u32[]{:S(2)}) collective-permute-start(f32[112,8,128]{2,1,0:T(8,128)S(1)} %get-tuple-element.54), channel_id=1, source_target_pairs={{0,1},{1,2},{2,3},{3,4},{4,5},{5,6},{6,7},{7,0},{8,9},{9,10},{10,1... | collective-permute-start | bytes 1376264 | tf_op jit(solution)/shard_map/ppermute | solution.py:44
  56.1 2.1 %collective-permute-start.17 = (f32[112,8,128]{2,1,0:T(8,128)S(1)}, f32[112,8,128]{2,1,0:T(8,128)S(1)}, u32[]{:S(2)}, u32[]{:S(2)}) collective-permute-start(f32[112,8,128]{2,1,0:T(8,128)S(1)} %get-tuple-element.55), channel_id=1, source_target_pairs={{0,7},{1,0},{2,1},{3,2},{4,3},{5,4},{6,5},{7,6},{8,15},{9,8},{10,9... | collective-permute-start | bytes 1376264 | tf_op jit(solution)/shard_map/ppermute | solution.py:45
  58.1 0.8 gram_rows.5.refs_5_
  59.0 4.3 %filter_orbitals.6.refs_2_ = f32[8,8,16,128]{3,2,1,0:T(8,128)S(1)} custom-call(f32[256,8,128]{2,1,0:T(8,128)S(1)} %collective-permute-done.refs_0_.lo_ref, f32[256,8,128]{2,1,0:T(8,128)S(1)} %get-tuple-element.31.refs_1_.mid_ref, f32[256,8,128]{2,1,0:T(8,128)S(1)} %collective-permute-done.1.refs_2_.hi_ref, ...), custom_call_target="tpu_custom_call" | custom-call | bytes 100 | tf_op jit(solution)/shard_map/filter_orbitals/pallas_call | solution.py:307
  63.3 1.1 %gram_rows.6.refs_6_ = f32[8,128]{1,0:T(8,128)S(1)} custom-call(f32[8,8,16,128]{3,2,1,0:T(8,128)S(1)} %get-tuple-element.40.refs_0_, f32[8,8,16,128]{3,2,1,0:T(8,128)S(1)} %filter_orbitals.5.refs_1_, f32[8,8,16,128]{3,2,1,0:T(8,128)S(1)} %filter_orbitals.6.refs_2_), custom_call_target="tpu_custom_call" | custom-call | bytes 100 | tf_op jit(solution)/shard_map/gram_rows/pallas_call | solution.py:375
  64.5 4.1 %filter_orbitals.7.refs_3_ = f32[8,8,16,128]{3,2,1,0:T(8,128)S(1)} custom-call(f32[128,8,128]{2,1,0:T(8,128)S(1)} %collective-permute-done.10.refs_0_.lo_ref, f32[128,8,128]{2,1,0:T(8,128)S(1)} %get-tuple-element.41.refs_1_.mid_ref, f32[128,8,128]{2,1,0:T(8,128)S(1)} %collective-permute-done.11.refs_2_.hi_ref, ...), custom_call_target="tpu_custom_call" | custom-call | bytes 100 | tf_op jit(solution)/shard_map/filter_orbitals/pallas_call | solution.py:307
  68.6 1.4 %gram_rows.7 = f32[8,128]{1,0:T(8,128)S(1)} custom-call(f32[8,8,16,128]{3,2,1,0:T(8,128)S(1)} %get-tuple-element.40.refs_0_, f32[8,8,16,128]{3,2,1,0:T(8,128)S(1)} %filter_orbitals.5.refs_1_, f32[8,8,16,128]{3,2,1,0:T(8,128)S(1)} %filter_orbitals.6.refs_2_, f32[8,8,16,128]{3,2,1,0:T(8,128)S(1)} %filter_orbitals.7.refs_3_, f32[8,128]{1,0:T(8,128)S(1)} %gram_rows.4.refs_4_, ...), custom_call_target="tpu_custom_call" | custom-call | bytes 100 | tf_op jit(solution)/shard_map/gram_rows/pallas_call | solution.py:375
  70.0 0.3 collective-permute-start.18
  70.3 1.0 %collective-permute-done.18 = f32[8,128]{1,0:T(8,128)S(1)} collective-permute-done((f32[8,128]{1,0:T(8,128)S(1)}, f32[8,128]{1,0:T(8,128)S(1)}, u32[]{:S(2)}, u32[]{:S(2)}) %collective-permute-start.18) | collective-permute-done | bytes 4128 | tf_op jit(solution)/shard_map/ppermute | solution.py:507
  71.3 21.1 %all_to_all.5.recv_ref = f32[64,8,128]{2,1,0:T(8,128)S(1)} all-to-all(f32[64,8,128]{2,1,0:T(8,128)S(1)} %broadcast_in_dim.2), channel_id=1, replica_groups=mesh['gx'=16,'gz'=4,'core'=2] {'gx','gz'}, dimensions={0} | all-to-all | bytes 524288 | tf_op jit(solution)/shard_map/all_to_all | solution.py:509
  92.5 3.9 %orthonormalize.1 = f32[32,8,16,128]{3,2,1,0:T(8,128)} custom-call(f32[64,8,128]{2,1,0:T(8,128)S(1)} %all_to_all.5.recv_ref, f32[8,8,16,128]{3,2,1,0:T(8,128)S(1)} %get-tuple-element.40.refs_0_, f32[8,8,16,128]{3,2,1,0:T(8,128)S(1)} %filter_orbitals.5.refs_1_, f32[8,8,16,128]{3,2,1,0:T(8,128)S(1)} %filter_orbitals.6.refs_2_, ...), custom_call_target="tpu_custom_call" | custom-call | tf_op jit(solution)/shard_map/orthonormalize/pallas_call | solution.py:441
  (32 shorter events, 0.5 us)
Async XLA Ops:
  0.0 7.5 %copy-start = (f32[32,8,16,128]{3,2,1,0:T(8,128)S(1)}, f32[32,8,16,128]{3,2,1,0:T(8,128)}, u32[]{:S(2)}) copy-start(f32[32,8,16,128]{3,2,1,0:T(8,128)} %orb_ref.3) | copy-start | bytes 6291460
  0.0 7.5 %copy-start.1 = (f32[8,16,128]{2,1,0:T(8,128)S(1)}, f32[8,16,128]{2,1,0:T(8,128)}, u32[]{:S(2)}) copy-start(f32[8,16,128]{2,1,0:T(8,128)} %pot_ref.3) | copy-start | bytes 196612
  2.0 19.8 %collective-permute-start.4 = (f32[144,8,128]{2,1,0:T(8,128)}, f32[144,8,128]{2,1,0:T(8,128)S(1)}, u32[]{:S(2)}, u32[]{:S(2)}) collective-permute-start(f32[144,8,128]{2,1,0:T(8,128)} %first_tiles.1), channel_id=1, source_target_pairs={{0,8},{8,16},{16,24},{24,32},{32,40},{40,48},{48,56},{56,64},{64,7... | collective-permute-start | bytes 1769480 | tf_op jit(solution)/shard_map/ppermute | solution.py:44
  3.7 18.1 %collective-permute-start.5 = (f32[144,8,128]{2,1,0:T(8,128)}, f32[144,8,128]{2,1,0:T(8,128)S(1)}, u32[]{:S(2)}, u32[]{:S(2)}) collective-permute-start(f32[144,8,128]{2,1,0:T(8,128)} %first_tiles.1), channel_id=1, source_target_pairs={{0,120},{8,0},{16,8},{24,16},{32,24},{40,32},{48,40},{56,48},{64,5... | collective-permute-start | bytes 1769480 | tf_op jit(solution)/shard_map/ppermute | solution.py:45
  8.0 7.3 %collective-permute-start.6 = (f32[64,8,128]{2,1,0:T(8,128)S(1)}, f32[64,8,128]{2,1,0:T(8,128)S(1)}, u32[]{:S(2)}, u32[]{:S(2)}) collective-permute-start(f32[64,8,128]{2,1,0:T(8,128)S(1)} %bitcast.11), channel_id=1, source_target_pairs={{0,1},{1,2},{2,3},{3,4},{4,5},{5,6},{6,7},{7,0},{8,9},{9,10},{10,1... | collective-permute-start | bytes 786440 | tf_op jit(solution)/shard_map/ppermute | solution.py:44
  8.0 36.3 %collective-permute-start = (f32[256,8,128]{2,1,0:T(8,128)S(1)}, f32[256,8,128]{2,1,0:T(8,128)S(1)}, u32[]{:S(2)}, u32[]{:S(2)}) collective-permute-start(f32[256,8,128]{2,1,0:T(8,128)S(1)} %get-tuple-element.31.refs_1_.mid_ref), channel_id=1, source_target_pairs={{0,8},{8,16},{16,24},{24,32},{32,40},{40,48},{48,56},{56,64},{64,7... | collective-permute-start | bytes 3145736 | tf_op jit(solution)/shard_map/ppermute | solution.py:44
  8.1 36.2 %collective-permute-start.1 = (f32[256,8,128]{2,1,0:T(8,128)S(1)}, f32[256,8,128]{2,1,0:T(8,128)S(1)}, u32[]{:S(2)}, u32[]{:S(2)}) collective-permute-start(f32[256,8,128]{2,1,0:T(8,128)S(1)} %get-tuple-element.31.refs_1_.mid_ref), channel_id=1, source_target_pairs={{0,120},{8,0},{16,8},{24,16},{32,24},{40,32},{48,40},{56,48},{64,5... | collective-permute-start | bytes 3145736 | tf_op jit(solution)/shard_map/ppermute | solution.py:45
  15.2 4.7 %collective-permute-start.7 = (f32[64,8,128]{2,1,0:T(8,128)S(1)}, f32[64,8,128]{2,1,0:T(8,128)S(1)}, u32[]{:S(2)}, u32[]{:S(2)}) collective-permute-start(f32[64,8,128]{2,1,0:T(8,128)S(1)} %bitcast.10), channel_id=1, source_target_pairs={{0,7},{1,0},{2,1},{3,2},{4,3},{5,4},{6,5},{7,6},{8,15},{9,8},{10,9... | collective-permute-start | bytes 786440 | tf_op jit(solution)/shard_map/ppermute | solution.py:45
  19.9 7.5 %collective-permute-start.2 = (f32[64,8,128]{2,1,0:T(8,128)S(1)}, f32[64,8,128]{2,1,0:T(8,128)S(1)}, u32[]{:S(2)}, u32[]{:S(2)}) collective-permute-start(f32[64,8,128]{2,1,0:T(8,128)S(1)} %bitcast.9), channel_id=1, source_target_pairs={{0,1},{1,2},{2,3},{3,4},{4,5},{5,6},{6,7},{7,0},{8,9},{9,10},{10,1... | collective-permute-start | bytes 786440 | tf_op jit(solution)/shard_map/ppermute | solution.py:44
  21.9 8.3 %collective-permute-start.8 = (f32[64,8,128]{2,1,0:T(8,128)S(1)}, f32[64,8,128]{2,1,0:T(8,128)S(1)}, u32[]{:S(2)}, u32[]{:S(2)}) collective-permute-start(f32[64,8,128]{2,1,0:T(8,128)S(1)} %get-tuple-element.35), channel_id=1, source_target_pairs={{0,1},{1,2},{2,3},{3,4},{4,5},{5,6},{6,7},{7,0},{8,9},{9,10},{10,1... | collective-permute-start | bytes 786440 | tf_op jit(solution)/shard_map/ppermute | solution.py:44
  21.9 12.4 %collective-permute-start.9 = (f32[64,8,128]{2,1,0:T(8,128)S(1)}, f32[64,8,128]{2,1,0:T(8,128)S(1)}, u32[]{:S(2)}, u32[]{:S(2)}) collective-permute-start(f32[64,8,128]{2,1,0:T(8,128)S(1)} %get-tuple-element.36), channel_id=1, source_target_pairs={{0,7},{1,0},{2,1},{3,2},{4,3},{5,4},{6,5},{7,6},{8,15},{9,8},{10,9... | collective-permute-start | bytes 786440 | tf_op jit(solution)/shard_map/ppermute | solution.py:45
  27.4 27.4 %collective-permute-start.10 = (f32[128,8,128]{2,1,0:T(8,128)S(1)}, f32[128,8,128]{2,1,0:T(8,128)S(1)}, u32[]{:S(2)}, u32[]{:S(2)}) collective-permute-start(f32[128,8,128]{2,1,0:T(8,128)S(1)} %get-tuple-element.41.refs_1_.mid_ref), channel_id=1, source_target_pairs={{0,8},{8,16},{16,24},{24,32},{32,40},{40,48},{48,56},{56,64},{64,7... | collective-permute-start | bytes 1572872 | tf_op jit(solution)/shard_map/ppermute | solution.py:44
  30.2 24.6 %collective-permute-start.11 = (f32[128,8,128]{2,1,0:T(8,128)S(1)}, f32[128,8,128]{2,1,0:T(8,128)S(1)}, u32[]{:S(2)}, u32[]{:S(2)}) collective-permute-start(f32[128,8,128]{2,1,0:T(8,128)S(1)} %get-tuple-element.41.refs_1_.mid_ref), channel_id=1, source_target_pairs={{0,120},{8,0},{16,8},{24,16},{32,24},{40,32},{48,40},{56,48},{64,5... | collective-permute-start | bytes 1572872 | tf_op jit(solution)/shard_map/ppermute | solution.py:45
  34.3 4.6 %collective-permute-start.3 = (f32[64,8,128]{2,1,0:T(8,128)S(1)}, f32[64,8,128]{2,1,0:T(8,128)S(1)}, u32[]{:S(2)}, u32[]{:S(2)}) collective-permute-start(f32[64,8,128]{2,1,0:T(8,128)S(1)} %bitcast.8), channel_id=1, source_target_pairs={{0,7},{1,0},{2,1},{3,2},{4,3},{5,4},{6,5},{7,6},{8,15},{9,8},{10,9... | collective-permute-start | bytes 786440 | tf_op jit(solution)/shard_map/ppermute | solution.py:45
  44.3 6.3 %collective-permute-start.12 = (f32[48,8,128]{2,1,0:T(8,128)S(1)}, f32[48,8,128]{2,1,0:T(8,128)S(1)}, u32[]{:S(2)}, u32[]{:S(2)}) collective-permute-start(f32[48,8,128]{2,1,0:T(8,128)S(1)} %get-tuple-element.44), channel_id=1, source_target_pairs={{0,1},{1,2},{2,3},{3,4},{4,5},{5,6},{6,7},{7,0},{8,9},{9,10},{10,1... | collective-permute-start | bytes 589832 | tf_op jit(solution)/shard_map/ppermute | solution.py:44
  44.3 6.3 %collective-permute-start.13 = (f32[48,8,128]{2,1,0:T(8,128)S(1)}, f32[48,8,128]{2,1,0:T(8,128)S(1)}, u32[]{:S(2)}, u32[]{:S(2)}) collective-permute-start(f32[48,8,128]{2,1,0:T(8,128)S(1)} %get-tuple-element.45), channel_id=1, source_target_pairs={{0,7},{1,0},{2,1},{3,2},{4,3},{5,4},{6,5},{7,6},{8,15},{9,8},{10,9... | collective-permute-start | bytes 589832 | tf_op jit(solution)/shard_map/ppermute | solution.py:45
  47.4 11.6 %collective-permute-start.14 = (f32[112,8,128]{2,1,0:T(8,128)S(1)}, f32[112,8,128]{2,1,0:T(8,128)S(1)}, u32[]{:S(2)}, u32[]{:S(2)}) collective-permute-start(f32[112,8,128]{2,1,0:T(8,128)S(1)} %get-tuple-element.50), channel_id=1, source_target_pairs={{0,1},{1,2},{2,3},{3,4},{4,5},{5,6},{6,7},{7,0},{8,9},{9,10},{10,1... | collective-permute-start | bytes 1376264 | tf_op jit(solution)/shard_map/ppermute | solution.py:44
  50.6 8.3 %collective-permute-start.15 = (f32[112,8,128]{2,1,0:T(8,128)S(1)}, f32[112,8,128]{2,1,0:T(8,128)S(1)}, u32[]{:S(2)}, u32[]{:S(2)}) collective-permute-start(f32[112,8,128]{2,1,0:T(8,128)S(1)} %get-tuple-element.51), channel_id=1, source_target_pairs={{0,7},{1,0},{2,1},{3,2},{4,3},{5,4},{6,5},{7,6},{8,15},{9,8},{10,9... | collective-permute-start | bytes 1376264 | tf_op jit(solution)/shard_map/ppermute | solution.py:45
  54.9 9.6 %collective-permute-start.16 = (f32[112,8,128]{2,1,0:T(8,128)S(1)}, f32[112,8,128]{2,1,0:T(8,128)S(1)}, u32[]{:S(2)}, u32[]{:S(2)}) collective-permute-start(f32[112,8,128]{2,1,0:T(8,128)S(1)} %get-tuple-element.54), channel_id=1, source_target_pairs={{0,1},{1,2},{2,3},{3,4},{4,5},{5,6},{6,7},{7,0},{8,9},{9,10},{10,1... | collective-permute-start | bytes 1376264 | tf_op jit(solution)/shard_map/ppermute | solution.py:44
  56.1 8.4 %collective-permute-start.17 = (f32[112,8,128]{2,1,0:T(8,128)S(1)}, f32[112,8,128]{2,1,0:T(8,128)S(1)}, u32[]{:S(2)}, u32[]{:S(2)}) collective-permute-start(f32[112,8,128]{2,1,0:T(8,128)S(1)} %get-tuple-element.55), channel_id=1, source_target_pairs={{0,7},{1,0},{2,1},{3,2},{4,3},{5,4},{6,5},{7,6},{8,15},{9,8},{10,9... | collective-permute-start | bytes 1376264 | tf_op jit(solution)/shard_map/ppermute | solution.py:45
  70.0 1.2 %collective-permute-start.18 = (f32[8,128]{1,0:T(8,128)S(1)}, f32[8,128]{1,0:T(8,128)S(1)}, u32[]{:S(2)}, u32[]{:S(2)}) collective-permute-start(f32[8,128]{1,0:T(8,128)S(1)} %gram_rows.7), channel_id=1, source_target_pairs={{0,1},{1,0},{2,3},{3,2},{4,5},{5,4},{6,7},{7,6},{8,9},{9,8},{10,11... | collective-permute-start | bytes 12296 | tf_op jit(solution)/shard_map/ppermute | solution.py:507
